TPU v7x, 256 devices: a whole 4x4x8 slice. The times are simulated.
256 devices in a mesh: section: 8 (over z), expert: 32 (over x, y, core).
Axes of the slice: x: 4, y: 4, z: 8, core: 2. Of those that a mesh axis runs over, the one named last changes fastest.
Arguments:
- out_grad: bfloat16 [8, 4096, 2560], P('section', 'expert'), may hold values from -6 to 6
- expert_ids: int32 [8, 4096], P('section', 'expert'), may hold values from 0 to 3, as said below
- slot_ids: int32 [8, 4096], P('section', 'expert'), may hold values from 0 to 32, as said below
- router_logits: float32 [8, 4096, 4], P('section', 'expert'), may hold values from -8 to 8
- saved_routed: bfloat16 [8, 32, 1056, 1024], P('section', 'expert'), may hold values from -6 to 6
- w_gate_up: bfloat16 [8, 32, 2560, 1024], P('section', 'expert'), may hold values from -0.125 to 0.125
- w_down: bfloat16 [8, 32, 512, 2560], P('section', 'expert'), may hold values from -0.09375 to 0.09375
- w_router: bfloat16 [8, 2560, 4], P('section'), may hold values from -0.125 to 0.125
Outputs:
- prev_grad: bfloat16 [8, 4096, 2560], P('section', 'expert')
- routed_hgrad: bfloat16 [8, 32, 1056, 1024], P('section', 'expert')
Inputs may be any that keep to these rules, and one draw needn't show every extreme that they name: `expert_ids`: in each aligned block of 128 tokens of a section (one device's), one expert is named by exactly 33 tokens and every other expert by 1 to 32 tokens. `slot_ids`: within a block of 128 tokens, the number of earlier tokens of the block with the same expert.
All inputs are finite; a program needn't handle non-finite values.
Results may differ from a plain program's by a relative error of at most 0.0062.
Values may be sent and summed in bfloat16 or wider, within the bound.
A program may use at most 128 MiB of HBM per device.

v0:
```python
import jax
import jax.numpy as jnp
from jax import lax
from jax.sharding import PartitionSpec as P


def shifted(value, axis, steps):
    count = lax.axis_size(axis)
    leading, last = (max(0, -steps), min(count, count - steps))
    return lax.ppermute(value, axis, [(source, source + steps) for source in range(leading, last)])


def silu_parts(gate_value):
    sigm = jax.nn.sigmoid(gate_value)
    return (gate_value * sigm, sigm * (1.0 + gate_value * (1.0 - sigm)))


def routed_backward(slot_rows, slot_score, kept, gate_up, down):
    half = down.shape[0]
    gate_value = kept[:, :half].astype(jnp.float32)
    up_value = kept[:, half:].astype(jnp.float32)
    activated, slope = silu_parts(gate_value)
    hidden = (activated * up_value).astype(jnp.bfloat16)
    expert_out = jnp.dot(hidden, down, preferred_element_type=jnp.float32)
    inner_dot = jnp.sum(slot_rows.astype(jnp.float32) * expert_out, axis=1).astype(jnp.bfloat16)
    hidden_grad = slot_score.astype(jnp.float32)[:, None] * lax.dot_general(
        slot_rows, down, (((1,), (1,)), ((), ())), preferred_element_type=jnp.float32
    )
    hidden_grads = jnp.concatenate(
        [
            (hidden_grad * up_value * slope).astype(jnp.bfloat16),
            (hidden_grad * activated).astype(jnp.bfloat16),
        ],
        axis=1,
    )
    slot_dx = lax.dot_general(
        hidden_grads, gate_up, (((1,), (1,)), ((), ())), preferred_element_type=jnp.float32
    ).astype(jnp.bfloat16)
    return (slot_dx, inner_dot, hidden_grads)


def on_device(
    out_grad, expert_ids, slot_ids, router_logits, saved_routed, w_gate_up, w_down, w_router
):
    upstream = out_grad[0]
    routes = expert_ids[0]
    places = slot_ids[0]
    logits = router_logits[0]
    kept_routed = saved_routed[0, 0]
    pieces_total = lax.axis_size("expert")
    expert_count = logits.shape[1]
    group = pieces_total // expert_count
    capacity = kept_routed.shape[0]
    per_peer = capacity // pieces_total
    features = upstream.shape[1]
    target = routes * per_peer + places
    onehot = routes[:, None] == jnp.arange(expert_count, dtype=jnp.int32)[None, :]
    chosen = jnp.sum(jnp.where(onehot, logits, jnp.float32(0.0)), axis=1)
    gate_prob = jax.nn.sigmoid(chosen)
    gating = gate_prob.astype(jnp.bfloat16)
    local_rows = (
        jnp.zeros((expert_count * per_peer, features), jnp.bfloat16).at[target].set(upstream)
    )
    local_score = jnp.zeros((expert_count * per_peer,), jnp.bfloat16).at[target].set(gating)
    send_rows = jnp.broadcast_to(
        local_rows.reshape(expert_count, 1, per_peer, features),
        (expert_count, group, per_peer, features),
    ).reshape(pieces_total, per_peer, features)
    send_score = jnp.broadcast_to(
        local_score.reshape(expert_count, 1, per_peer), (expert_count, group, per_peer)
    ).reshape(pieces_total, per_peer)
    recv_rows, recv_score = (
        lax.all_to_all(send_rows, "expert", split_axis=0, concat_axis=0, tiled=True),
        lax.all_to_all(send_score, "expert", split_axis=0, concat_axis=0, tiled=True),
    )
    slot_dx, inner_dot, hidden_grads = routed_backward(
        recv_rows.reshape(capacity, features),
        recv_score.reshape(capacity),
        kept_routed,
        w_gate_up[0, 0],
        w_down[0, 0],
    )
    outgoing = (
        slot_dx.reshape(pieces_total, per_peer, features),
        inner_dot.reshape(pieces_total, per_peer),
    )
    rows_part = lax.all_to_all(outgoing[0], "expert", split_axis=0, concat_axis=0, tiled=True)
    inner_part = lax.all_to_all(outgoing[1], "expert", split_axis=0, concat_axis=0, tiled=True)
    count = rows_part.shape[1]
    rows_sum = jnp.sum(
        rows_part.astype(jnp.float32).reshape(expert_count, group, count, features), axis=1
    )
    inner_sum = jnp.sum(inner_part.astype(jnp.float32).reshape(expert_count, group, count), axis=1)
    flat_rows = rows_sum.reshape(expert_count * per_peer, features)
    flat_inner = inner_sum.reshape(expert_count * per_peer)
    returned = flat_rows[target]
    inner_tok = flat_inner[target]
    dlogit = gate_prob * (1.0 - gate_prob) * inner_tok
    coeffs = jnp.where(onehot, dlogit[:, None], jnp.float32(0.0))
    router_dx = jnp.dot(coeffs, w_router[0].astype(jnp.float32).T, precision=lax.Precision.HIGHEST)
    summed = (returned + router_dx).astype(jnp.bfloat16)
    previous = shifted(summed, "section", -1)
    return (previous[None], hidden_grads[None, None])


def solution(mesh):
    placed = (
        P("section", "expert", None),
        P("section", "expert"),
        P("section", "expert"),
        P("section", "expert", None),
        P("section", "expert", None, None),
        P("section", "expert", None, None),
        P("section", "expert", None, None),
        P("section", None, None),
    )
    return jax.shard_map(
        on_device,
        mesh=mesh,
        in_specs=placed,
        out_specs=(P("section", "expert", None), P("section", "expert", None, None)),
        check_vma=False,
    )
```

profile of v0, /device:TPU:64, one launch (start us, length us, event | category | flops | bytes accessed | tf_op | source)
XLA Modules:
  0.0 289.8 jit_solution(12562523334257827291)
XLA Ops:
  0.6 0.0 copy-start
  0.6 0.8 fusion.28
  1.5 2.9 %scatter_custom_fusion.1 = bf16[132,2560]{1,0:T(8,128)(2,1)} fusion(s32[128]{0:T(128)S(1)} %fusion.28, bf16[1,128,2560]{2,1,0:T(8,128)(2,1)} %param.8, bf16[]{:T(256)} %constant.6.clone.1), kind=kCustom, calls=%fused_computation.31 | custom fusion | bytes 1331202 | tf_op jit(solution)/shard_map/scatter | solution.py:62
  4.4 1.3 broadcast_in_dim.52
  5.7 3.2 %broadcast_in_dim.53 = bf16[4,8,33,2560]{3,2,1,0:T(8,128)(2,1)} broadcast(bf16[4,33,2560]{2,1,0:T(8,128)(2,1)S(1)} %broadcast_in_dim.52), dimensions={0,2,3} | broadcast | bytes 6082560 | tf_op jit(solution)/shard_map/broadcast_in_dim | solution.py:65
  8.9 0.0 copy-start.5
  8.9 0.0 copy-start.6
  8.9 7.6 %all-to-all-start.1 = ((bf16[32,33,2560]{2,1,0:T(8,128)(2,1)}), bf16[32,33,2560]{2,1,0:T(8,128)(2,1)}, u32[]{:S(2)}, u32[]{:S(2)}) async-start(bf16[32,33,2560]{2,1,0:T(8,128)(2,1)} %bitcast.43), calls=%async_computation.1 | async-start | bytes 13107200 | tf_op jit(solution)/shard_map/all_to_all | solution.py:73
  16.5 0.0 copy-done.5
  16.5 0.0 copy-done.6
  16.5 84.3 %all-to-all-done.1 = bf16[32,33,2560]{2,1,0:T(8,128)(2,1)} async-done(((bf16[32,33,2560]{2,1,0:T(8,128)(2,1)}), bf16[32,33,2560]{2,1,0:T(8,128)(2,1)}, u32[]{:S(2)}, u32[]{:S(2)}) %all-to-all-start.1) | async-done | bytes 5406752 | tf_op jit(solution)/shard_map/all_to_all | solution.py:73
  100.8 6.3 %reshape.106 = bf16[1056,2560]{1,0:T(8,128)(2,1)} reshape(bf16[32,33,2560]{2,1,0:T(8,128)(2,1)} %all-to-all-done.1) | data formatting | bytes 10813440 | tf_op jit(solution)/shard_map/reshape | solution.py:77
  107.1 0.0 copy-done
  107.1 6.6 %fusion.4 = bf16[1056]{0:T(1024)(128)(2,1)S(1)} fusion(bf16[1,1,512,2560]{3,2,1,0:T(8,128)(2,1)S(1)} %copy-done, bf16[1056,2560]{1,0:T(8,128)(2,1)} %reshape.106, bf16[1056,1024]{1,0:T(8,128)(2,1)} %bitcast.48), kind=kOutput, calls=%fused_computation.18 | convolution fusion | flops 2780675072 | bytes 10192960 | tf_op jit(solution)/shard_map/dot_general | solution.py:24
  113.8 0.7 convert_element_type.81
  114.5 18.2 %all-to-all-start.3 = ((bf16[32,1,33]{2,1,0:T(2,128)(2,1)}), bf16[32,1,33]{2,1,0:T(2,128)(2,1)S(1)}, u32[]{:S(2)}, u32[]{:S(2)}) async-start(bf16[32,1,33]{2,1,0:T(2,128)(2,1)} %convert_element_type.81), calls=%async_computation.3 | async-start | bytes 32768 | tf_op jit(solution)/shard_map/all_to_all | solution.py:88
  132.7 7.3 %all-to-all-done.3 = bf16[32,1,33]{2,1,0:T(2,128)(2,1)S(1)} async-done(((bf16[32,1,33]{2,1,0:T(2,128)(2,1)}), bf16[32,1,33]{2,1,0:T(2,128)(2,1)S(1)}, u32[]{:S(2)}, u32[]{:S(2)}) %all-to-all-start.3) | async-done | bytes 2144 | tf_op jit(solution)/shard_map/all_to_all | solution.py:88
  140.1 0.1 reshape.111
  140.1 1.3 gather_fusion.1
  141.4 1.3 scatter_custom_fusion
  142.8 0.1 broadcast_in_dim.49
  142.9 10.7 %all_to_all.25 = bf16[32,1,33]{2,1,0:T(2,128)(2,1)S(1)} all-to-all(bf16[32,1,33]{2,1,0:T(2,128)(2,1)S(1)} %copy.11), channel_id=1, replica_groups=mesh['section'=8,'expert'=32] {'expert'}, dimensions={0} | all-to-all | bytes 4224 | tf_op jit(solution)/shard_map/all_to_all | solution.py:74
  153.6 0.1 convert_reduce_fusion.1
  153.6 0.1 reshape.112
  153.7 6.7 %fusion.8 = (bf16[1056,512]{1,0:T(8,128)(2,1)S(1)}, bf16[1056,512]{1,0:T(8,128)(2,1)S(1)}) fusion(bf16[1056,1024]{1,0:T(8,128)(2,1)} %bitcast.49, bf16[1056,2560]{1,0:T(8,128)(2,1)} %reshape.106, bf16[1,1,512,2560]{3,2,1,0:T(8,128)(2,1)S(1)} %copy-done, f32[1056]{0:T(1024)S(1)} %reshape.112), kind=kOutput, calls=%fused_computation.20 | convolution fusion | flops 2776891392 | bytes 12357760 | tf_op jit(solution)/shard_map/dot_general | solution.py:26
  160.5 0.0 copy-start.1
  160.5 0.0 copy-start.3
  160.5 1.0 copy-done.1
  161.5 0.4 copy-done.3
  161.9 10.1 %convolution_convert_fusion = bf16[1056,2560]{1,0:T(8,128)(2,1)} fusion(bf16[1,1,2560,1024]{3,2,1,0:T(8,128)(2,1)} %param.13, bf16[1056,512]{1,0:T(8,128)(2,1)S(1)} %get-tuple-element.5, bf16[1056,512]{1,0:T(8,128)(2,1)S(1)} %get-tuple-element.4), kind=kOutput, calls=%fused_computation.6 | convolution fusion | flops 5543510016 | bytes 12812288 | tf_op jit(solution)/shard_map/dot_general | solution.py:36
  172.1 6.4 %reshape.107 = bf16[32,33,2560]{2,1,0:T(8,128)(2,1)} reshape(bf16[1056,2560]{1,0:T(8,128)(2,1)} %convolution_convert_fusion) | data formatting | bytes 10813440 | tf_op jit(solution)/shard_map/reshape | solution.py:84
  178.4 80.4 %all_to_all.26 = bf16[32,33,2560]{2,1,0:T(8,128)(2,1)S(1)} all-to-all(bf16[32,33,2560]{2,1,0:T(8,128)(2,1)} %reshape.107), channel_id=1, replica_groups=mesh['section'=8,'expert'=32] {'expert'}, dimensions={0} | all-to-all | bytes 10813440 | tf_op jit(solution)/shard_map/all_to_all | solution.py:87
  258.9 2.1 convert_reduce_fusion
  261.0 2.7 reshape.110
  263.8 0.0 copy-start.4
  263.8 4.0 %gather_fusion = f32[128,2560]{1,0:T(8,128)} fusion(f32[132,2560]{1,0:T(8,128)} %reshape.110, s32[1024]{0:T(1024)S(1)} %pad_clamp_fusion), kind=kCustom, calls=%fused_computation | custom fusion | bytes 2621952 | tf_op jit(solution)/shard_map/gather | solution.py:96
  267.7 0.0 copy-start.2
  267.7 0.0 copy-done.4
  267.8 2.2 fusion.1
  269.9 2.0 collective-permute-start
  271.9 0.0 copy-done.2
  271.9 2.8 fusion.15
  274.7 14.2 %collective-permute-done = bf16[128,2560]{1,0:T(8,128)(2,1)S(1)} collective-permute-done((bf16[128,2560]{1,0:T(8,128)(2,1)S(1)}, bf16[128,2560]{1,0:T(8,128)(2,1)S(1)}, u32[]{:S(2)}, u32[]{:S(2)}) %collective-permute-start) | collective-permute-done | bytes 655392 | tf_op jit(solution)/shard_map/ppermute | solution.py:10
  288.9 0.8 copy.14
  (7 shorter events, 0.1 us)
Async XLA Ops:
  0.6 106.5 %copy-start = (bf16[1,1,512,2560]{3,2,1,0:T(8,128)(2,1)S(1)}, bf16[1,1,512,2560]{3,2,1,0:T(8,128)(2,1)}, u32[]{:S(2)}) copy-start(bf16[1,1,512,2560]{3,2,1,0:T(8,128)(2,1)} %param.14) | copy-start | bytes 7864324
  8.9 7.6 %copy-start.5 = (s32[1,128]{1,0:T(1,128)S(1)}, s32[1,128]{1,0:T(1,128)}, u32[]{:S(2)}) copy-start(s32[1,128]{1,0:T(1,128)} %param.9) | copy-start | bytes 1540
  8.9 7.6 %copy-start.6 = (f32[1,128,4]{1,2,0:T(4,128)S(1)}, f32[1,128,4]{1,2,0:T(4,128)}, u32[]{:S(2)}) copy-start(f32[1,128,4]{1,2,0:T(4,128)} %param.11) | copy-start | bytes 6148
  8.9 91.9 %all-to-all-start.1 = ((bf16[32,33,2560]{2,1,0:T(8,128)(2,1)}), bf16[32,33,2560]{2,1,0:T(8,128)(2,1)}, u32[]{:S(2)}, u32[]{:S(2)}) async-start(bf16[32,33,2560]{2,1,0:T(8,128)(2,1)} %bitcast.43), calls=%async_computation.1 | async-start | bytes 13107200 | tf_op jit(solution)/shard_map/all_to_all | solution.py:73
  114.5 25.5 %all-to-all-start.3 = ((bf16[32,1,33]{2,1,0:T(2,128)(2,1)}), bf16[32,1,33]{2,1,0:T(2,128)(2,1)S(1)}, u32[]{:S(2)}, u32[]{:S(2)}) async-start(bf16[32,1,33]{2,1,0:T(2,128)(2,1)} %convert_element_type.81), calls=%async_computation.3 | async-start | bytes 32768 | tf_op jit(solution)/shard_map/all_to_all | solution.py:88
  160.5 1.0 copy-start.1
  160.5 1.4 copy-start.3
  263.8 4.0 %copy-start.4 = (bf16[1,2560,4]{1,2,0:T(4,128)(2,1)S(1)}, bf16[1,2560,4]{1,2,0:T(4,128)(2,1)}, u32[]{:S(2)}) copy-start(bf16[1,2560,4]{1,2,0:T(4,128)(2,1)} %param.15) | copy-start | bytes 61444
  267.7 4.2 %copy-start.2 = (bf16[1056,512]{1,0:T(8,128)(2,1)S(1)}, bf16[1056,512]{1,0:T(8,128)(2,1)}, u32[]{:S(2)}) copy-start(bf16[1056,512]{1,0:T(8,128)(2,1)} %copy-done.1) | copy-start | bytes 3244036
  269.9 19.0 %collective-permute-start = (bf16[128,2560]{1,0:T(8,128)(2,1)S(1)}, bf16[128,2560]{1,0:T(8,128)(2,1)S(1)}, u32[]{:S(2)}, u32[]{:S(2)}) collective-permute-start(bf16[128,2560]{1,0:T(8,128)(2,1)S(1)} %fusion.1), channel_id=1, source_target_pairs={{32,0},{64,32},{96,64},{128,96},{160,128},{192,160},{224,192},{33,... | collective-permute-start | bytes 1966088 | tf_op jit(solution)/shard_map/ppermute | solution.py:10
where the time goes:
time: 292 us; the launch traced here: 290 us
  waiting for transfers between devices  106 us (36%)
  blocking collectives  91.1 us (31%)
  local copies, waits for them, and re-layouts  32.8 us (11%)
  starting transfers between devices  27.8 us (10%)
  matrix products  25.7 us (9%)
  other arithmetic  5.92 us (2%)
    all_to_all x1, waiting for transfers between devices, on_device(): lax.all_to_all(send_rows, 'expert', split_axis=0, concat_axis=0, tiled=True)  84.3 us
    all_to_all x1, blocking collectives, on_device(): lax.all_to_all(outgoing[0], 'expert', split_axis=0, concat_axis=0, tiled=...  80.4 us
    all_to_all x1, starting transfers between devices, on_device(): lax.all_to_all(outgoing[1], 'expert', split_axis=0, concat_axis=0, tiled=...  18.2 us
    ppermute x1, waiting for transfers between devices, shifted(): lax.ppermute(value, axis, [(source, source + steps) for source in range(l...  14.2 us
    all_to_all x1, blocking collectives, on_device(): lax.all_to_all(send_score, 'expert', split_axis=0, concat_axis=0, tiled=T...  10.7 us
    dot_general x1, matrix products, routed_backward(): lax.dot_general(hidden_grads, gate_up, (((1,), (1,)), ((), ())), preferre...  10.1 us
    all_to_all x1, starting transfers between devices, on_device(): lax.all_to_all(send_rows, 'expert', split_axis=0, concat_axis=0, tiled=True)  7.57 us
    all_to_all x1, waiting for transfers between devices, on_device(): lax.all_to_all(outgoing[1], 'expert', split_axis=0, concat_axis=0, tiled=...  7.27 us
  transfers between devices with their start and end apart: 3, of which 3 were waited for; matrix products, arithmetic and copies ran while one was open for 1% of the time, Pallas kernels for 0%

commit v1 on v0

v1 whole, which is shorter than its diff:
```python
import jax
import jax.numpy as jnp
from jax import lax
from jax.experimental import pallas as pl
from jax.experimental.pallas import tpu as pltpu
from jax.sharding import PartitionSpec as P

F32, BF16, I32 = jnp.float32, jnp.bfloat16, jnp.int32
SIDE = 4
TOK = 128
MOST = 33
REG = 32
D = 2560
FF_DEV = 512
SLOTS = 1056
QUART = D // 4
TILE_W = QUART + 128
WIN = 48

ORDER = [(0, 0), (0, 1), (0, 3), (0, 2), (3, 0), (1, 0), (3, 1), (1, 3), (2, 0), (1, 2), (2, 1), (2, 3), (3, 3), (2, 2), (3, 2), (1, 1)]
SLOT = {chunk: i for i, chunk in enumerate(ORDER)}
STEPS = 8
PLUS = (0, 1)


def packed(values):
    return sum(v << (2 * i) for i, v in enumerate(values))


PACK = [[packed([ORDER[2 * i + j][axis] for i in range(STEPS)]) for j in range(2)] for axis in range(2)]


def dot(a, b):
    return lax.dot_general(a, b, (((1,), (0,)), ((), ())), preferred_element_type=F32)


def dot_t(a, b):
    return lax.dot_general(a, b, (((1,), (1,)), ((), ())), preferred_element_type=F32)


def iota(shape, axis):
    return lax.broadcasted_iota(I32, shape, axis)


def onehot(mask):
    return jnp.where(mask, F32(1.0), F32(0.0)).astype(BF16)


def to_column(row, rows):
    mask = iota((rows, 128), 0) == iota((rows, 128), 1)
    return jnp.sum(jnp.where(mask, row, jnp.zeros((), row.dtype)), axis=1, keepdims=True)


def to_row(column):
    shape = (column.shape[0], 128)
    mask = iota(shape, 0) == iota(shape, 1)
    return jnp.sum(jnp.where(mask, column, jnp.zeros((), column.dtype)), axis=0, keepdims=True)


def backward(g, score, kept):
    gate_value, up_value = kept[:, :FF_DEV], kept[:, FF_DEV:]
    sigm = jax.nn.sigmoid(gate_value)
    activated = gate_value * sigm
    slope = sigm * (1.0 + gate_value * (1.0 - sigm))
    hidden = (activated * up_value).astype(BF16).astype(F32)
    inner = jnp.sum(hidden * g, axis=1, keepdims=True)
    hidden_grad = score * g
    hg = jnp.concatenate([hidden_grad * up_value * slope, hidden_grad * activated], axis=1).astype(BF16)
    return hg, inner


def kernel(sections, up_ref, ids_ref, slots_ref, logits_ref, router_ref, kept_hbm, wgu_hbm, wd_hbm,
           prev_ref, hgrad_hbm,
           kept_v, wgu_v, wd_v, hgo_v, x_v, xs_v, es_v, ein_v, eall_v, own_v, sbo_v, sbi_v, out_v,
           rel_v, dir_v, rto_v, rti_v, inn_v, fin_v, fino_v, ft_v, fto_v, rt_v, rts_v, hg_v, wrow_v, kex_v,
           send_sem, recv_sem, sb_send, sb_recv, loc_sem):
    sec = lax.axis_index("section")
    me = lax.axis_index("expert")
    c = lax.rem(me, 2)
    y = lax.rem(me // 2, SIDE)
    x = me // (2 * SIDE)

    def dev(dx=0, dy=0, dc=0, dz=0):
        s = lax.rem(sec + dz + sections, sections)
        e = (lax.rem(x + dx + SIDE, SIDE) * SIDE + lax.rem(y + dy + SIDE, SIDE)) * 2 + lax.rem(c + dc, 2)
        return (s, e)

    table = {}
    for d in (1, 3, 2):
        table["x", d] = (xs_v.at[d - 1], x_v.at[SLOT[0, d], 0], dev(dx=-d))
        table["e", d] = (es_v.at[d], ein_v.at[d - 1], dev(dx=-d))
    for d in range(4):
        n0 = SLOT[0, d]
        table["y+", d] = (x_v.at[n0, 0], x_v.at[SLOT[3, d], 0], dev(dy=1))
        table["y-", d] = (x_v.at[n0, 0], x_v.at[SLOT[1, d], 0], dev(dy=-1))
        if d in PLUS:
            table["yr", d] = (x_v.at[SLOT[3, d], 0], x_v.at[SLOT[2, d], 0], dev(dy=1))
            table["rr", d] = (out_v.at[SLOT[2, d]], rel_v.at[d], dev(dy=1))
        else:
            table["yr", d] = (x_v.at[SLOT[1, d], 0], x_v.at[SLOT[2, d], 0], dev(dy=-1))
            table["rr", d] = (out_v.at[SLOT[2, d]], rel_v.at[d], dev(dy=-1))
        for k in range(4):
            n = SLOT[k, d]
            table["sib", k, d] = (x_v.at[n, 0], x_v.at[n, 1], dev(dc=1))
        table["d+", d] = (out_v.at[SLOT[1, d]], dir_v.at[0, d], dev(dy=1))
        table["d-", d] = (out_v.at[SLOT[3, d]], dir_v.at[1, d], dev(dy=-1))
        table["f", d] = (fino_v.at[d], fin_v.at[d], dev(dx=d, dz=-1))
        table["ft", d] = (fto_v, ft_v.at[d], dev(dx=d, dz=-1))
    for i in range(1, 8):
        k, s = i // 2, i % 2
        j = 2 * ((4 - k) % 4) + s
        table["ea", i] = (eall_v.at[0], eall_v.at[j], dev(dy=k, dc=s))
        table["rt", i] = (rto_v.at[i], rti_v.at[j], dev(dy=k, dc=s))
    table[("ids",)] = (rts_v, rt_v, dev(dz=-1))
    number = {name: i for i, name in enumerate(table)}

    def copy(*name):
        src, dst, device = table[name]
        i = number[name]
        return pltpu.make_async_remote_copy(
            src_ref=src, dst_ref=dst, send_sem=send_sem.at[i], recv_sem=recv_sem.at[i],
            device_id=device, device_id_type=pl.DeviceIdType.MESH)

    def start(*name):
        copy(*name).start()

    def recv(*name):
        copy(*name).wait_recv()

    kept_copy = pltpu.make_async_copy(kept_hbm, kept_v, loc_sem.at[0])
    wd_copy = pltpu.make_async_copy(wd_hbm, wd_v, loc_sem.at[1])
    wgu_copy = pltpu.make_async_copy(wgu_hbm, wgu_v, loc_sem.at[2])
    wd_copy.start()
    kept_copy.start()
    wgu_copy.start()

    barrier = pltpu.get_barrier_semaphore()
    partners = [dev(dx=d) for d in (1, 2, 3)]
    partners += [dev(dy=k, dc=s) for k in range(4) for s in range(2) if k or s]
    partners += [dev(dx=d, dz=dz) for d in range(4) for dz in (-1, 1)]
    for partner in partners:
        pl.semaphore_signal(barrier, inc=1, device_id=partner, device_id_type=pl.DeviceIdType.MESH)

    ids_row, slot_row = ids_ref[...], slots_ref[...]
    rel_row = jnp.bitwise_and(x + SIDE - ids_row, 3)
    key = jnp.where(slot_row < REG, rel_row * REG + slot_row, -1)
    perm = onehot(iota((TOK, TOK), 0) == key)
    up = up_ref[...]
    rows = dot(perm, up).astype(BF16)
    x_v[SLOT[0, 0], 0] = rows[:REG]
    for d in range(1, 4):
        xs_v[d - 1] = rows[d * REG:(d + 1) * REG]
    ids_col, slot_col = to_column(ids_row, TOK), to_column(slot_row, TOK)
    chosen = jnp.sum(jnp.where(iota((TOK, SIDE), 1) == ids_col, logits_ref[...], 0.0), axis=1, keepdims=True)
    part = jax.nn.sigmoid(chosen)
    fold = jnp.zeros((4 * 16, QUART), F32)
    gates = jnp.zeros((4 * 16, 128), F32)
    for q in range(4):
        place = iota((4 * 16, TOK), 0) == rel_row * 17 + 4 * q
        fold += dot(onehot(place & (slot_row == REG)), up[:, q * QUART:(q + 1) * QUART])
        if q < 3:
            rounded = part.astype(BF16).astype(F32)
            spread = jnp.where(iota((TOK, 128), 1) == slot_col, rounded, 0.0).astype(BF16)
            gates += dot(onehot(place), spread)
            part = part - rounded
    tiles = jnp.concatenate([fold, gates], axis=1).astype(BF16)
    for d in range(4):
        es_v[d] = tiles[16 * d:16 * (d + 1)]
    rts_v[...] = jnp.concatenate([ids_row, slot_row, jnp.zeros((6, TOK), I32)], axis=0)

    pl.semaphore_wait(barrier, len(partners))
    for d in (1, 3):
        start("x", d)
    for d in (1, 2, 3):
        start("e", d)
    start("x", 2)
    start("y+", 0)
    start("y-", 0)
    start("sib", 0, 0)
    start("ids")

    chosen_expert = onehot(iota((8, SIDE), 1) == x)
    wrow_v[...] = dot_t(chosen_expert, router_ref[...])
    inn_v[...] = jnp.zeros_like(inn_v)

    @pl.loop(0, SLOTS // WIN)
    def _(i):
        hgo_v[pl.ds(pl.multiple_of(i * WIN, 16), WIN), :] = jnp.zeros((WIN, 2 * FF_DEV), BF16)

    for d in (1, 2, 3):
        recv("e", d)
    tile = es_v[0].astype(F32)
    for d in (1, 2, 3):
        tile += ein_v[d - 1].astype(F32)
    eall_v[0] = tile.astype(BF16)
    for i in range(1, 8):
        start("ea", i)

    def extra_row(shape, axis):
        r = iota(shape, axis)
        idx, d = r // 4, jnp.bitwise_and(r, 3)
        b = jnp.bitwise_and(x + d, 3) * 8 + jnp.bitwise_and(y + idx // 2, 3) * 2 + jnp.bitwise_and(c + idx, 1)
        return b * MOST + REG

    kept_copy.wait()

    def gather_kept(i, total):
        window = kept_v[pl.ds(pl.multiple_of(i * WIN, 16), WIN), :]
        return total + dot(onehot(iota((32, WIN), 1) + i * WIN == extra_row((32, WIN), 0)), window)

    kex_v[...] = lax.fori_loop(0, SLOTS // WIN, gather_kept, jnp.zeros((32, 2 * FF_DEV), F32))
    wd_copy.wait()
    wgu_copy.wait()

    before = [
        [("recv", "x", 1), ("start", "y+", 1), ("start", "sib", 0, 1), ("recv", "x", 3), ("start", "y-", 3), ("start", "sib", 0, 3)]
        + [("recv", "ea", i) for i in range(1, 8)],
        [("recv", "x", 2), ("start", "y-", 2), ("start", "sib", 0, 2),
         ("recv", "y+", 0), ("start", "yr", 0), ("start", "sib", 3, 0), ("recv", "y-", 0), ("start", "sib", 1, 0)],
        [("recv", "y+", 1), ("start", "yr", 1), ("start", "sib", 3, 1), ("recv", "y-", 3), ("start", "yr", 3), ("start", "sib", 1, 3),
         ("start", "y+", 3), ("start", "y+", 2)],
        [],
        [("recv", "y-", 2), ("start", "yr", 2), ("start", "sib", 1, 2), ("start", "y-", 1), ("recv", "yr", 0), ("start", "sib", 2, 0)],
        [("recv", "yr", 1), ("start", "sib", 2, 1), ("recv", "yr", 3), ("start", "sib", 2, 3)],
        [("recv", "y+", 3), ("start", "sib", 3, 3), ("recv", "yr", 2), ("start", "sib", 2, 2)],
        [("recv", "y+", 2), ("start", "sib", 3, 2), ("recv", "y-", 1), ("start", "sib", 1, 1)],
    ]
    after = [[], [], [("d-", 0)], [("d-", 1), ("d+", 3)], [("rr", 0), ("d+", 2)], [("rr", 1), ("rr", 3)], [("rr", 2)], []]

    def half_copy(n):
        return pltpu.make_async_remote_copy(
            src_ref=sbo_v.at[n], dst_ref=sbi_v.at[n], send_sem=sb_send.at[n], recv_sem=sb_recv.at[n],
            device_id=dev(dc=1), device_id_type=pl.DeviceIdType.MESH)

    def finish(m):
        for j in range(2):
            n = 2 * m + j
            half_copy(n).wait_recv()
            both = own_v[n] + sbi_v[n].astype(F32)
            own_v[n] = both
            out_v[n] = both.astype(BF16)

    @pl.loop(0, STEPS)
    def _(it):
        for i in range(STEPS):
            @pl.when(it == i)
            def _():
                for act, *name in before[i]:
                    (recv if act == "recv" else start)(*name)
                for j in range(2):
                    recv("sib", *ORDER[2 * i + j])

        rows = x_v[pl.ds(2 * it, 2)].reshape(4 * REG, D)
        g = dot_t(rows, wd_v[...])
        for j in range(2):
            k, d = [jnp.bitwise_and(jnp.right_shift(jnp.int32(PACK[axis][j]), 2 * it), 3) for axis in range(2)]
            for s in range(2):
                at = (2 * j + s) * REG
                idx = 2 * k + s
                first = (jnp.bitwise_and(x + d, 3) * 8 + jnp.bitwise_and(y + k, 3) * 2 + jnp.bitwise_and(c + s, 1)) * MOST
                base = pl.multiple_of(first // 16 * 16, 16)
                off = first - base
                window = pl.ds(base, WIN)
                kept = dot(onehot(iota((REG, WIN), 1) == iota((REG, WIN), 0) + off), kept_v[window, :])
                line = iota((16, 128), 0) == d
                score_row = jnp.sum(jnp.where(line, eall_v[idx, :, QUART:].astype(F32), 0.0), axis=0, keepdims=True)
                hg, inner = backward(g[at:at + REG], to_column(score_row, REG), kept)
                hg_v[at:at + REG, :] = hg
                inn_v[idx] = jnp.where(line, to_row(inner), inn_v[idx])
                placed = dot(onehot(iota((WIN, REG), 0) == iota((WIN, REG), 1) + off), hg)
                hgo_v[window, :] = (hgo_v[window, :].astype(F32) + placed).astype(BF16)
        for t in range(5):
            cols = slice(512 * t, 512 * (t + 1))
            dx = dot_t(hg_v[...], wgu_v[cols, :])
            for j in range(2):
                own_v[2 * it + j, :, cols] = dx[2 * j * REG:(2 * j + 1) * REG]
                sbo_v[2 * it + j, :, cols] = dx[(2 * j + 1) * REG:(2 * j + 2) * REG].astype(BF16)
        for j in range(2):
            half_copy(2 * it + j).start()

        @pl.when(it > 0)
        def _():
            finish(it - 1)
            for i in range(STEPS):
                if after[i]:
                    @pl.when(it - 1 == i)
                    def _():
                        for name in after[i]:
                            start(*name)

    finish(STEPS - 1)

    spread_tiles = eall_v[...].reshape(8 * 16, TILE_W)

    def select(q, flip):
        shape = (128, 32) if flip else (32, 128)
        r, place = iota(shape, 1 if flip else 0), iota(shape, 0 if flip else 1)
        return onehot(place == r // 4 * 16 + 4 * q + jnp.bitwise_and(r, 3))

    extra = jnp.concatenate([dot(select(q, False), spread_tiles[:, :QUART]).astype(BF16) for q in range(4)], axis=1)
    gate_rows = dot(select(0, False), spread_tiles[:, QUART:])
    score = jnp.sum(jnp.where(iota((32, 128), 1) == REG, gate_rows, 0.0), axis=1, keepdims=True)
    hg, inner = backward(dot_t(extra, wd_v[...]), score, kex_v[...])
    folded = jnp.zeros((8 * 16, QUART), F32)
    for q in range(4):
        folded += dot(select(q, True), dot_t(hg, wgu_v[q * QUART:(q + 1) * QUART, :]).astype(BF16))
    inner_at = jnp.where(iota((32, 128), 1) == REG, inner, 0.0).astype(BF16)
    inners = inn_v[...].reshape(8 * 16, 128) + dot(select(0, True), inner_at)
    rto_v[...] = jnp.concatenate([folded, inners], axis=1).astype(BF16).reshape(8, 16, TILE_W)
    for i in range(1, 8):
        start("rt", i)

    for d in (0, 3, 1, 2):
        recv("rr", d)
        n = SLOT[1 if d in PLUS else 3, d]
        out_v[n] = (own_v[n] + rel_v[d].astype(F32)).astype(BF16)
        start("d+" if d in PLUS else "d-", d)

    @pl.loop(0, SLOTS // WIN)
    def _(i):
        window = pl.ds(pl.multiple_of(i * WIN, 16), WIN)
        placed = dot(onehot(iota((WIN, 32), 0) + i * WIN == extra_row((WIN, 32), 1)), hg)
        hgo_v[window, :] = (hgo_v[window, :].astype(F32) + placed).astype(BF16)

    hgrad_copy = pltpu.make_async_copy(hgo_v, hgrad_hbm, loc_sem.at[3])
    hgrad_copy.start()

    total = rto_v[0].astype(F32)
    for i in range(1, 8):
        recv("rt", i)
    for i in range(1, 8):
        total += rti_v[i].astype(F32)
    gate_tile = eall_v[0, :, QUART:].astype(F32)
    kind = jnp.bitwise_and(iota((16, 128), 0), 3)
    terms = []
    for d in range(4):
        gate = jnp.sum(jnp.where(kind == d, gate_tile, 0.0), axis=0, keepdims=True)
        inner_row = jnp.sum(jnp.where(iota((16, 128), 0) == d, total[:, QUART:], 0.0), axis=0, keepdims=True)
        terms.append(gate * (1.0 - gate) * inner_row)
    all_terms = jnp.zeros((16, 128), F32)
    for d in range(4):
        all_terms = jnp.where(kind == d, terms[d], all_terms)
    last_term = jnp.sum(jnp.where(iota((16, 128), 1) == REG, all_terms, 0.0), axis=1, keepdims=True)
    w_row = wrow_v[0:1, :]
    w_fold = jnp.zeros((16, QUART), F32)
    for q in range(4):
        w_fold = jnp.where(iota((16, QUART), 0) // 4 == q, w_row[:, q * QUART:(q + 1) * QUART], w_fold)
    fto_v[...] = (total[:, :QUART] + last_term * w_fold).astype(BF16)
    for d in range(4):
        start("ft", d)
    for d in (0, 3, 1, 2):
        recv("d+", d)
        recv("d-", d)
        n = SLOT[0, d]
        rows = own_v[n] + dir_v[0, d].astype(F32) + dir_v[1, d].astype(F32)
        fino_v[d] = (rows + to_column(terms[d], REG) * w_row).astype(BF16)
        start("f", d)

    recv("ids")
    ids_col, slot_col = to_column(rt_v[0:1, :], TOK), to_column(rt_v[1:2, :], TOK)
    live = sec < sections - 1
    rel_col = jnp.bitwise_and(x + SIDE - ids_col, 3)
    back = onehot((iota((TOK, TOK), 1) == jnp.where(slot_col < REG, rel_col * REG + slot_col, -1)) & live)
    for d in range(4):
        recv("ft", d)
    for d in (0, 3, 1, 2):
        recv("f", d)
    fins = fin_v[...].reshape(TOK, D)
    fts = ft_v[...].reshape(4 * 16, QUART)
    for q in range(4):
        cols = slice(q * QUART, (q + 1) * QUART)
        pick = onehot((iota((TOK, 4 * 16), 1) == jnp.where(slot_col == REG, rel_col * 17 + 4 * q, -1)) & live)
        prev_ref[:, cols] = (dot(back, fins[:, cols]) + dot(pick, fts)).astype(BF16)

    for name in table:
        copy(*name).wait_send()
    for n in range(2 * STEPS):
        half_copy(n).wait_send()
    hgrad_copy.wait()


def on_device(out_grad, expert_ids, slot_ids, router_logits, saved_routed, w_gate_up, w_down, w_router):
    sections = lax.axis_size("section")
    vmem = pl.BlockSpec(memory_space=pltpu.VMEM)
    hbm = pl.BlockSpec(memory_space=pl.ANY)

    def body(*refs):
        kernel(sections, *refs)

    count = 3 + 3 + 4 * 10 + 16 + 14 + 1
    prev, hgrad = pl.pallas_call(
        body,
        out_shape=(jax.ShapeDtypeStruct((TOK, D), BF16), jax.ShapeDtypeStruct((SLOTS, 2 * FF_DEV), BF16)),
        in_specs=[vmem] * 5 + [hbm] * 3,
        out_specs=(vmem, hbm),
        scratch_shapes=[
            pltpu.VMEM((SLOTS, 2 * FF_DEV), BF16),
            pltpu.VMEM((D, 2 * FF_DEV), BF16),
            pltpu.VMEM((FF_DEV, D), BF16),
            pltpu.VMEM((SLOTS, 2 * FF_DEV), BF16),
            pltpu.VMEM((16, 2, REG, D), BF16),
            pltpu.VMEM((3, REG, D), BF16),
            pltpu.VMEM((4, 16, TILE_W), BF16),
            pltpu.VMEM((3, 16, TILE_W), BF16),
            pltpu.VMEM((8, 16, TILE_W), BF16),
            pltpu.VMEM((16, REG, D), F32),
            pltpu.VMEM((16, REG, D), BF16),
            pltpu.VMEM((16, REG, D), BF16),
            pltpu.VMEM((16, REG, D), BF16),
            pltpu.VMEM((4, REG, D), BF16),
            pltpu.VMEM((2, 4, REG, D), BF16),
            pltpu.VMEM((8, 16, TILE_W), BF16),
            pltpu.VMEM((8, 16, TILE_W), BF16),
            pltpu.VMEM((8, 16, 128), F32),
            pltpu.VMEM((4, REG, D), BF16),
            pltpu.VMEM((4, REG, D), BF16),
            pltpu.VMEM((4, 16, QUART), BF16),
            pltpu.VMEM((16, QUART), BF16),
            pltpu.VMEM((8, TOK), I32),
            pltpu.VMEM((8, TOK), I32),
            pltpu.VMEM((4 * REG, 2 * FF_DEV), BF16),
            pltpu.VMEM((8, D), F32),
            pltpu.VMEM((32, 2 * FF_DEV), F32),
            pltpu.SemaphoreType.DMA((count,)),
            pltpu.SemaphoreType.DMA((count,)),
            pltpu.SemaphoreType.DMA((16,)),
            pltpu.SemaphoreType.DMA((16,)),
            pltpu.SemaphoreType.DMA((4,)),
        ],
        compiler_params=pltpu.CompilerParams(collective_id=0, has_side_effects=True, vmem_limit_bytes=60 * 2**20),
        cost_estimate=pl.CostEstimate(flops=9 * 10**9, bytes_accessed=14 * 10**6, transcendentals=600000),
    )(out_grad[0], expert_ids, slot_ids, router_logits[0], w_router[0], saved_routed[0, 0], w_gate_up[0, 0], w_down[0, 0])
    return prev[None], hgrad[None, None]


def solution(mesh):
    placed = (
        P("section", "expert", None),
        P("section", "expert"),
        P("section", "expert"),
        P("section", "expert", None),
        P("section", "expert", None, None),
        P("section", "expert", None, None),
        P("section", "expert", None, None),
        P("section", None, None),
    )
    return jax.shard_map(
        on_device,
        mesh=mesh,
        in_specs=placed,
        out_specs=(P("section", "expert", None), P("section", "expert", None, None)),
        check_vma=False,
    )
```

time: 292 us -> 101 us (0.35)
  waiting for transfers between devices: 106 us -> 0 us
  Pallas kernels: 0 us -> 91.2 us
  blocking collectives: 91.1 us -> 0 us
  starting transfers between devices: 27.8 us -> 0 us
  matrix products: 25.7 us -> 0 us
  local copies, waits for them, and re-layouts: 32.8 us -> 8.37 us
  other arithmetic: 5.92 us -> 0 us
    all_to_all x2 -> x0, waiting for transfers between devices: 91.6 us -> none  [the longest x1 84.3 us: on_device(): lax.all_to_all(send_rows, 'expert', split_axis=0, concat_axis=0, tiled=True)]
    pallas_call x0 -> x1, Pallas kernels: none -> 91.2 us  [on_device(): pl.pallas_call(body, out_shape=(jax.ShapeDtypeStruct((TOK, D), BF16), jax...]
    all_to_all x2 -> x0, blocking collectives: 91.1 us -> none  [the longest x1 80.4 us: on_device(): lax.all_to_all(outgoing[0], 'expert', split_axis=0, concat_axis=0, tiled=...]
    all_to_all x2 -> x0, starting transfers between devices: 25.8 us -> none  [the longest x1 18.2 us: on_device(): lax.all_to_all(outgoing[1], 'expert', split_axis=0, concat_axis=0, tiled=...]
    dot_general x4 -> x0, matrix products: 25.7 us -> none  [the longest x1 10.1 us: routed_backward(): lax.dot_general(hidden_grads, gate_up, (((1,), (1,)), ((), ())), preferre...]
    reshape x4 -> x0, local copies, waits for them, and re-layouts: 15.6 us -> none  [the longest x1 6.39 us: on_device(): slot_dx.reshape(pieces_total, per_peer, features)]
    ppermute x1 -> x0, waiting for transfers between devices: 14.2 us -> none  [shifted(): lax.ppermute(value, axis, [(source, source + steps) for source in range(l...]
    unnamed x15 -> x4, local copies, waits for them, and re-layouts: 2.28 us -> 8.37 us
  transfers between devices with their start and end apart: 3 -> 0, of which waited for: 3 -> 0; matrix products, arithmetic and copies ran while one was open for 1% -> 0% of each run, Pallas kernels for 0% -> 0%
where the time goes in v1:
time: 101 us; the launch traced here: 100 us
  Pallas kernels  91.2 us (90%)
  local copies, waits for them, and re-layouts  8.37 us (8%)
    pallas_call x1, Pallas kernels, on_device(): pl.pallas_call(body, out_shape=(jax.ShapeDtypeStruct((TOK, D), BF16), jax...  91.2 us
    unnamed x4, local copies, waits for them, and re-layouts  8.37 us

profile of v1, /device:TPU:64, one launch (start us, length us, event | category | flops | bytes accessed | tf_op | source)
XLA Modules:
  0.0 100.2 jit_solution(14193693568129864790)
XLA Ops:
  0.6 1.4 %copy.10 = f32[1,128,4]{2,1,0:T(8,128)} copy(f32[1,128,4]{1,2,0:T(4,128)} %param.11) | data formatting | bytes 4096 | tf_op args[3]
  2.0 1.9 %copy.11 = bf16[1,2560,4]{2,1,0:T(8,128)(2,1)} copy(bf16[1,2560,4]{1,2,0:T(4,128)(2,1)} %param.15) | data formatting | bytes 40960 | tf_op args[7]
  3.9 91.2 %shard_map.95 = (bf16[128,2560]{1,0:T(8,128)(2,1)}, bf16[1056,1024]{1,0:T(8,128)(2,1)}) custom-call(bf16[128,2560]{1,0:T(8,128)(2,1)} %bitcast.15, s32[1,128]{1,0:T(1,128)} %refs_1_.1, s32[1,128]{1,0:T(1,128)} %refs_2_.1, f32[128,4]{1,0:T(8,128)} %bitcast.11, bf16[2560,4]{1,0:T(8,128)(2,1)} %bitcast.10, bf16[1056,1024]{1,0:T(8,128)(2,1)} %bitcast.14, ...), custom_call_target="tpu_custom_call" | custom-call | flops 8999999488 | bytes 14000000 | tf_op jit(solution)/shard_map/pallas_call | solution.py:391
  95.1 2.0 %copy.14 = bf16[1,128,2560]{2,1,0:T(8,128)(2,1)} copy(bf16[1,128,2560]{2,1,0:T(8,128)(2,1)} %bitcast.9) | data formatting | bytes 1310720
  97.1 3.1 %copy.15 = bf16[1,1,1056,1024]{3,2,1,0:T(8,128)(2,1)} copy(bf16[1,1,1056,1024]{3,2,1,0:T(8,128)(2,1)} %bitcast.8) | data formatting | bytes 4325376

commit v2 on v1

--- a/solution.py
+++ b/solution.py
@@ -15,7 +15,8 @@
 SLOTS = 1056
 QUART = D // 4
 TILE_W = QUART + 128
-WIN = 48
+HALF = D // 2
+PART = 528
 
 ORDER = [(0, 0), (0, 1), (0, 3), (0, 2), (3, 0), (1, 0), (3, 1), (1, 3), (2, 0), (1, 2), (2, 1), (2, 3), (3, 3), (2, 2), (3, 2), (1, 1)]
 SLOT = {chunk: i for i, chunk in enumerate(ORDER)}
@@ -32,10 +33,6 @@
 
 def dot(a, b):
     return lax.dot_general(a, b, (((1,), (0,)), ((), ())), preferred_element_type=F32)
-
-
-def dot_t(a, b):
-    return lax.dot_general(a, b, (((1,), (1,)), ((), ())), preferred_element_type=F32)
 
 
 def iota(shape, axis):
@@ -71,8 +68,8 @@
 
 def kernel(sections, up_ref, ids_ref, slots_ref, logits_ref, router_ref, kept_hbm, wgu_hbm, wd_hbm,
            prev_ref, hgrad_hbm,
-           kept_v, wgu_v, wd_v, hgo_v, x_v, xs_v, es_v, ein_v, eall_v, own_v, sbo_v, sbi_v, out_v,
-           rel_v, dir_v, rto_v, rti_v, inn_v, fin_v, fino_v, ft_v, fto_v, rt_v, rts_v, hg_v, wrow_v, kex_v,
+           kept_v, wgu_v, wd_v, wgut_v, wdt_v, perm_v, kp_v, hgp_v, x_v, xs_v, es_v, ein_v, eall_v, own_v, sbo_v, sbi_v, out_v,
+           rel_v, dir_v, rto_v, rti_v, inn_v, fin_v, fino_v, ft_v, fto_v, rt_v, rts_v, hg_v,
            send_sem, recv_sem, sb_send, sb_recv, loc_sem):
     sec = lax.axis_index("section")
     me = lax.axis_index("expert")
@@ -102,9 +99,10 @@
         for k in range(4):
             n = SLOT[k, d]
             table["sib", k, d] = (x_v.at[n, 0], x_v.at[n, 1], dev(dc=1))
-        table["d+", d] = (out_v.at[SLOT[1, d]], dir_v.at[0, d], dev(dy=1))
-        table["d-", d] = (out_v.at[SLOT[3, d]], dir_v.at[1, d], dev(dy=-1))
-        table["f", d] = (fino_v.at[d], fin_v.at[d], dev(dx=d, dz=-1))
+        for h in range(2):
+            table["d+", d, h] = (out_v.at[SLOT[1, d], h], dir_v.at[0, d, h], dev(dy=1))
+            table["d-", d, h] = (out_v.at[SLOT[3, d], h], dir_v.at[1, d, h], dev(dy=-1))
+            table["f", d, h] = (fino_v.at[d, h], fin_v.at[d, h], dev(dx=d, dz=-1))
         table["ft", d] = (fto_v, ft_v.at[d], dev(dx=d, dz=-1))
     for i in range(1, 8):
         k, s = i // 2, i % 2
@@ -151,8 +149,8 @@
     for d in range(1, 4):
         xs_v[d - 1] = rows[d * REG:(d + 1) * REG]
     ids_col, slot_col = to_column(ids_row, TOK), to_column(slot_row, TOK)
-    chosen = jnp.sum(jnp.where(iota((TOK, SIDE), 1) == ids_col, logits_ref[...], 0.0), axis=1, keepdims=True)
-    part = jax.nn.sigmoid(chosen)
+    chosen = jnp.sum(jnp.where(iota((SIDE, TOK), 0) == ids_row, logits_ref[...], 0.0), axis=0, keepdims=True)
+    part = to_column(jax.nn.sigmoid(chosen), TOK)
     fold = jnp.zeros((4 * 16, QUART), F32)
     gates = jnp.zeros((4 * 16, 128), F32)
     for q in range(4):
@@ -168,6 +166,11 @@
         es_v[d] = tiles[16 * d:16 * (d + 1)]
     rts_v[...] = jnp.concatenate([ids_row, slot_row, jnp.zeros((6, TOK), I32)], axis=0)
 
+    def capacity(p):
+        return jnp.where(p < 16 * REG, p // REG * MOST + jnp.bitwise_and(p, REG - 1), (p - 16 * REG) * MOST + REG)
+
+    perm_v[...] = onehot(capacity(iota((PART, PART), 0)) == iota((PART, PART), 1))
+    inn_v[...] = jnp.zeros_like(inn_v)
     pl.semaphore_wait(barrier, len(partners))
     for d in (1, 3):
         start("x", d)
@@ -179,14 +182,9 @@
     start("sib", 0, 0)
     start("ids")
 
-    chosen_expert = onehot(iota((8, SIDE), 1) == x)
-    wrow_v[...] = dot_t(chosen_expert, router_ref[...])
-    inn_v[...] = jnp.zeros_like(inn_v)
-
-    @pl.loop(0, SLOTS // WIN)
-    def _(i):
-        hgo_v[pl.ds(pl.multiple_of(i * WIN, 16), WIN), :] = jnp.zeros((WIN, 2 * FF_DEV), BF16)
-
+    wd_copy.wait()
+    for t in range(5):
+        wdt_v[512 * t:512 * (t + 1), :] = wd_v[:, 512 * t:512 * (t + 1)].T
     for d in (1, 2, 3):
         recv("e", d)
     tile = es_v[0].astype(F32)
@@ -196,36 +194,34 @@
     for i in range(1, 8):
         start("ea", i)
 
-    def extra_row(shape, axis):
-        r = iota(shape, axis)
-        idx, d = r // 4, jnp.bitwise_and(r, 3)
-        b = jnp.bitwise_and(x + d, 3) * 8 + jnp.bitwise_and(y + idx // 2, 3) * 2 + jnp.bitwise_and(c + idx, 1)
-        return b * MOST + REG
-
     kept_copy.wait()
-
-    def gather_kept(i, total):
-        window = kept_v[pl.ds(pl.multiple_of(i * WIN, 16), WIN), :]
-        return total + dot(onehot(iota((32, WIN), 1) + i * WIN == extra_row((32, WIN), 0)), window)
-
-    kex_v[...] = lax.fori_loop(0, SLOTS // WIN, gather_kept, jnp.zeros((32, 2 * FF_DEV), F32))
-    wd_copy.wait()
+    for p in range(2):
+        for t in range(2):
+            cols = slice(512 * t, 512 * (t + 1))
+            kp_v[p, :, cols] = dot(perm_v[...], kept_v[PART * p:PART * (p + 1), cols]).astype(BF16)
+    perm_v[...] = onehot(capacity(iota((PART, PART), 1)) == iota((PART, PART), 0))
+    for d, way in ((1, "y+"), (3, "y-")):
+        recv("x", d)
+        start(way, d)
+        start("sib", 0, d)
     wgu_copy.wait()
+    for t in range(5):
+        wgut_v[:, 512 * t:512 * (t + 1)] = wgu_v[512 * t:512 * (t + 1), :].T
 
     before = [
-        [("recv", "x", 1), ("start", "y+", 1), ("start", "sib", 0, 1), ("recv", "x", 3), ("start", "y-", 3), ("start", "sib", 0, 3)]
-        + [("recv", "ea", i) for i in range(1, 8)],
-        [("recv", "x", 2), ("start", "y-", 2), ("start", "sib", 0, 2),
-         ("recv", "y+", 0), ("start", "yr", 0), ("start", "sib", 3, 0), ("recv", "y-", 0), ("start", "sib", 1, 0)],
+        [("recv", "ea", 1)],
+        [("recv", "y+", 0), ("start", "yr", 0), ("start", "sib", 3, 0), ("recv", "y-", 0), ("start", "sib", 1, 0),
+         ("recv", "x", 2), ("start", "y-", 2), ("start", "sib", 0, 2)],
         [("recv", "y+", 1), ("start", "yr", 1), ("start", "sib", 3, 1), ("recv", "y-", 3), ("start", "yr", 3), ("start", "sib", 1, 3),
-         ("start", "y+", 3), ("start", "y+", 2)],
+         ("start", "y+", 3), ("start", "y+", 2)]
+        + [("recv", "ea", i) for i in range(2, 8)],
         [],
         [("recv", "y-", 2), ("start", "yr", 2), ("start", "sib", 1, 2), ("start", "y-", 1), ("recv", "yr", 0), ("start", "sib", 2, 0)],
         [("recv", "yr", 1), ("start", "sib", 2, 1), ("recv", "yr", 3), ("start", "sib", 2, 3)],
         [("recv", "y+", 3), ("start", "sib", 3, 3), ("recv", "yr", 2), ("start", "sib", 2, 2)],
         [("recv", "y+", 2), ("start", "sib", 3, 2), ("recv", "y-", 1), ("start", "sib", 1, 1)],
     ]
-    after = [[], [], [("d-", 0)], [("d-", 1), ("d+", 3)], [("rr", 0), ("d+", 2)], [("rr", 1), ("rr", 3)], [("rr", 2)], []]
+    after = [[], [], [], [], [("rr", 0)], [("rr", 1), ("rr", 3)], [("rr", 2)], []]
 
     def half_copy(n):
         return pltpu.make_async_remote_copy(
@@ -251,30 +247,26 @@
                     recv("sib", *ORDER[2 * i + j])
 
         rows = x_v[pl.ds(2 * it, 2)].reshape(4 * REG, D)
-        g = dot_t(rows, wd_v[...])
+        g = dot(rows, wdt_v[...])
         for j in range(2):
             k, d = [jnp.bitwise_and(jnp.right_shift(jnp.int32(PACK[axis][j]), 2 * it), 3) for axis in range(2)]
             for s in range(2):
                 at = (2 * j + s) * REG
                 idx = 2 * k + s
-                first = (jnp.bitwise_and(x + d, 3) * 8 + jnp.bitwise_and(y + k, 3) * 2 + jnp.bitwise_and(c + s, 1)) * MOST
-                base = pl.multiple_of(first // 16 * 16, 16)
-                off = first - base
-                window = pl.ds(base, WIN)
-                kept = dot(onehot(iota((REG, WIN), 1) == iota((REG, WIN), 0) + off), kept_v[window, :])
+                b = jnp.bitwise_and(x + d, 3) * 8 + jnp.bitwise_and(y + k, 3) * 2 + jnp.bitwise_and(c + s, 1)
+                window = pl.ds(pl.multiple_of(jnp.bitwise_and(b, 15) * REG, REG), REG)
+                kept = kp_v[b // 16, window, :].astype(F32)
                 line = iota((16, 128), 0) == d
                 score_row = jnp.sum(jnp.where(line, eall_v[idx, :, QUART:].astype(F32), 0.0), axis=0, keepdims=True)
                 hg, inner = backward(g[at:at + REG], to_column(score_row, REG), kept)
                 hg_v[at:at + REG, :] = hg
                 inn_v[idx] = jnp.where(line, to_row(inner), inn_v[idx])
-                placed = dot(onehot(iota((WIN, REG), 0) == iota((WIN, REG), 1) + off), hg)
-                hgo_v[window, :] = (hgo_v[window, :].astype(F32) + placed).astype(BF16)
-        for t in range(5):
-            cols = slice(512 * t, 512 * (t + 1))
-            dx = dot_t(hg_v[...], wgu_v[cols, :])
+                hgp_v[b // 16, window, :] = hg
+        for h in range(2):
+            dx = dot(hg_v[...], wgut_v[:, HALF * h:HALF * (h + 1)])
             for j in range(2):
-                own_v[2 * it + j, :, cols] = dx[2 * j * REG:(2 * j + 1) * REG]
-                sbo_v[2 * it + j, :, cols] = dx[(2 * j + 1) * REG:(2 * j + 2) * REG].astype(BF16)
+                own_v[2 * it + j, h] = dx[2 * j * REG:(2 * j + 1) * REG]
+                sbo_v[2 * it + j, h] = dx[(2 * j + 1) * REG:(2 * j + 2) * REG].astype(BF16)
         for j in range(2):
             half_copy(2 * it + j).start()
 
@@ -290,39 +282,54 @@
 
     finish(STEPS - 1)
 
+    def first_of(a, b, h):
+        start("d+", b, h)
+        start("d-", a, h)
+
+    def second_of(a, b, h):
+        for d, k, way in ((a, 1, "d+"), (b, 3, "d-")):
+            n = SLOT[k, d]
+            if h == 0:
+                recv("rr", d)
+            out_v[n, h] = (own_v[n, h] + rel_v[d, h].astype(F32)).astype(BF16)
+            start(way, d, h)
+
+    stages = [(0, 3, 0), (1, 2, 0), (0, 3, 1), (1, 2, 1)]
+    first_of(*stages[0])
+
     spread_tiles = eall_v[...].reshape(8 * 16, TILE_W)
 
     def select(q, flip):
         shape = (128, 32) if flip else (32, 128)
-        r, place = iota(shape, 1 if flip else 0), iota(shape, 0 if flip else 1)
-        return onehot(place == r // 4 * 16 + 4 * q + jnp.bitwise_and(r, 3))
+        b, place = iota(shape, 1 if flip else 0), iota(shape, 0 if flip else 1)
+        idx = 2 * jnp.bitwise_and(b // 2 - y + SIDE, 3) + jnp.bitwise_and(b + c, 1)
+        return onehot(place == idx * 16 + 4 * q + jnp.bitwise_and(b // 8 - x + SIDE, 3))
 
     extra = jnp.concatenate([dot(select(q, False), spread_tiles[:, :QUART]).astype(BF16) for q in range(4)], axis=1)
     gate_rows = dot(select(0, False), spread_tiles[:, QUART:])
     score = jnp.sum(jnp.where(iota((32, 128), 1) == REG, gate_rows, 0.0), axis=1, keepdims=True)
-    hg, inner = backward(dot_t(extra, wd_v[...]), score, kex_v[...])
+    kept = kp_v[:, 16 * REG:, :].reshape(32, 2 * FF_DEV).astype(F32)
+    hg, inner = backward(dot(extra, wdt_v[...]), score, kept)
+    hgp_v[:, 16 * REG:, :] = hg.reshape(2, 16, 2 * FF_DEV)
+    dx = dot(hg, wgut_v[...]).astype(BF16)
     folded = jnp.zeros((8 * 16, QUART), F32)
     for q in range(4):
-        folded += dot(select(q, True), dot_t(hg, wgu_v[q * QUART:(q + 1) * QUART, :]).astype(BF16))
+        folded += dot(select(q, True), dx[:, q * QUART:(q + 1) * QUART])
     inner_at = jnp.where(iota((32, 128), 1) == REG, inner, 0.0).astype(BF16)
     inners = inn_v[...].reshape(8 * 16, 128) + dot(select(0, True), inner_at)
     rto_v[...] = jnp.concatenate([folded, inners], axis=1).astype(BF16).reshape(8, 16, TILE_W)
     for i in range(1, 8):
         start("rt", i)
 
-    for d in (0, 3, 1, 2):
-        recv("rr", d)
-        n = SLOT[1 if d in PLUS else 3, d]
-        out_v[n] = (own_v[n] + rel_v[d].astype(F32)).astype(BF16)
-        start("d+" if d in PLUS else "d-", d)
-
-    @pl.loop(0, SLOTS // WIN)
-    def _(i):
-        window = pl.ds(pl.multiple_of(i * WIN, 16), WIN)
-        placed = dot(onehot(iota((WIN, 32), 0) + i * WIN == extra_row((WIN, 32), 1)), hg)
-        hgo_v[window, :] = (hgo_v[window, :].astype(F32) + placed).astype(BF16)
-
-    hgrad_copy = pltpu.make_async_copy(hgo_v, hgrad_hbm, loc_sem.at[3])
+    second_of(*stages[0])
+    first_of(*stages[1])
+    second_of(*stages[1])
+
+    for p in range(2):
+        for t in range(2):
+            cols = slice(512 * t, 512 * (t + 1))
+            kept_v[PART * p:PART * (p + 1), cols] = dot(perm_v[...], hgp_v[p, :, cols]).astype(BF16)
+    hgrad_copy = pltpu.make_async_copy(kept_v, hgrad_hbm, loc_sem.at[3])
     hgrad_copy.start()
 
     total = rto_v[0].astype(F32)
@@ -341,20 +348,24 @@
     for d in range(4):
         all_terms = jnp.where(kind == d, terms[d], all_terms)
     last_term = jnp.sum(jnp.where(iota((16, 128), 1) == REG, all_terms, 0.0), axis=1, keepdims=True)
-    w_row = wrow_v[0:1, :]
+    w_row = jnp.sum(jnp.where(iota((SIDE, D), 0) == x, router_ref[...].astype(F32), 0.0), axis=0, keepdims=True)
     w_fold = jnp.zeros((16, QUART), F32)
     for q in range(4):
         w_fold = jnp.where(iota((16, QUART), 0) // 4 == q, w_row[:, q * QUART:(q + 1) * QUART], w_fold)
     fto_v[...] = (total[:, :QUART] + last_term * w_fold).astype(BF16)
     for d in range(4):
         start("ft", d)
-    for d in (0, 3, 1, 2):
-        recv("d+", d)
-        recv("d-", d)
-        n = SLOT[0, d]
-        rows = own_v[n] + dir_v[0, d].astype(F32) + dir_v[1, d].astype(F32)
-        fino_v[d] = (rows + to_column(terms[d], REG) * w_row).astype(BF16)
-        start("f", d)
+    for i, (a, b, h) in enumerate(stages):
+        for d in (b, a):
+            recv("d+", d, h)
+            recv("d-", d, h)
+            n = SLOT[0, d]
+            rows = own_v[n, h] + dir_v[0, d, h].astype(F32) + dir_v[1, d, h].astype(F32)
+            fino_v[d, h] = (rows + to_column(terms[d], REG) * w_row[:, HALF * h:HALF * (h + 1)]).astype(BF16)
+            start("f", d, h)
+        if i + 2 < len(stages):
+            first_of(*stages[i + 2])
+            second_of(*stages[i + 2])
 
     recv("ids")
     ids_col, slot_col = to_column(rt_v[0:1, :], TOK), to_column(rt_v[1:2, :], TOK)
@@ -363,14 +374,15 @@
     back = onehot((iota((TOK, TOK), 1) == jnp.where(slot_col < REG, rel_col * REG + slot_col, -1)) & live)
     for d in range(4):
         recv("ft", d)
-    for d in (0, 3, 1, 2):
-        recv("f", d)
-    fins = fin_v[...].reshape(TOK, D)
     fts = ft_v[...].reshape(4 * 16, QUART)
-    for q in range(4):
-        cols = slice(q * QUART, (q + 1) * QUART)
-        pick = onehot((iota((TOK, 4 * 16), 1) == jnp.where(slot_col == REG, rel_col * 17 + 4 * q, -1)) & live)
-        prev_ref[:, cols] = (dot(back, fins[:, cols]) + dot(pick, fts)).astype(BF16)
+    for h in range(2):
+        for d in range(4):
+            recv("f", d, h)
+        whole = dot(back, fin_v[:, h].reshape(TOK, HALF))
+        for q in (2 * h, 2 * h + 1):
+            pick = onehot((iota((TOK, 4 * 16), 1) == jnp.where(slot_col == REG, rel_col * 17 + 4 * q, -1)) & live)
+            at = (q - 2 * h) * QUART
+            prev_ref[:, q * QUART:(q + 1) * QUART] = (whole[:, at:at + QUART] + dot(pick, fts)).astype(BF16)
 
     for name in table:
         copy(*name).wait_send()
@@ -387,7 +399,7 @@
     def body(*refs):
         kernel(sections, *refs)
 
-    count = 3 + 3 + 4 * 10 + 16 + 14 + 1
+    count = 96
     prev, hgrad = pl.pallas_call(
         body,
         out_shape=(jax.ShapeDtypeStruct((TOK, D), BF16), jax.ShapeDtypeStruct((SLOTS, 2 * FF_DEV), BF16)),
@@ -397,30 +409,32 @@
             pltpu.VMEM((SLOTS, 2 * FF_DEV), BF16),
             pltpu.VMEM((D, 2 * FF_DEV), BF16),
             pltpu.VMEM((FF_DEV, D), BF16),
-            pltpu.VMEM((SLOTS, 2 * FF_DEV), BF16),
+            pltpu.VMEM((2 * FF_DEV, D), BF16),
+            pltpu.VMEM((D, FF_DEV), BF16),
+            pltpu.VMEM((PART, PART), BF16),
+            pltpu.VMEM((2, PART, 2 * FF_DEV), BF16),
+            pltpu.VMEM((2, PART, 2 * FF_DEV), BF16),
             pltpu.VMEM((16, 2, REG, D), BF16),
             pltpu.VMEM((3, REG, D), BF16),
             pltpu.VMEM((4, 16, TILE_W), BF16),
             pltpu.VMEM((3, 16, TILE_W), BF16),
             pltpu.VMEM((8, 16, TILE_W), BF16),
-            pltpu.VMEM((16, REG, D), F32),
-            pltpu.VMEM((16, REG, D), BF16),
-            pltpu.VMEM((16, REG, D), BF16),
-            pltpu.VMEM((16, REG, D), BF16),
-            pltpu.VMEM((4, REG, D), BF16),
-            pltpu.VMEM((2, 4, REG, D), BF16),
+            pltpu.VMEM((16, 2, REG, HALF), F32),
+            pltpu.VMEM((16, 2, REG, HALF), BF16),
+            pltpu.VMEM((16, 2, REG, HALF), BF16),
+            pltpu.VMEM((16, 2, REG, HALF), BF16),
+            pltpu.VMEM((4, 2, REG, HALF), BF16),
+            pltpu.VMEM((2, 4, 2, REG, HALF), BF16),
             pltpu.VMEM((8, 16, TILE_W), BF16),
             pltpu.VMEM((8, 16, TILE_W), BF16),
             pltpu.VMEM((8, 16, 128), F32),
-            pltpu.VMEM((4, REG, D), BF16),
-            pltpu.VMEM((4, REG, D), BF16),
+            pltpu.VMEM((4, 2, REG, HALF), BF16),
+            pltpu.VMEM((4, 2, REG, HALF), BF16),
             pltpu.VMEM((4, 16, QUART), BF16),
             pltpu.VMEM((16, QUART), BF16),
             pltpu.VMEM((8, TOK), I32),
             pltpu.VMEM((8, TOK), I32),
             pltpu.VMEM((4 * REG, 2 * FF_DEV), BF16),
-            pltpu.VMEM((8, D), F32),
-            pltpu.VMEM((32, 2 * FF_DEV), F32),
             pltpu.SemaphoreType.DMA((count,)),
             pltpu.SemaphoreType.DMA((count,)),
             pltpu.SemaphoreType.DMA((16,)),
@@ -429,7 +443,7 @@
         ],
         compiler_params=pltpu.CompilerParams(collective_id=0, has_side_effects=True, vmem_limit_bytes=60 * 2**20),
         cost_estimate=pl.CostEstimate(flops=9 * 10**9, bytes_accessed=14 * 10**6, transcendentals=600000),
-    )(out_grad[0], expert_ids, slot_ids, router_logits[0], w_router[0], saved_routed[0, 0], w_gate_up[0, 0], w_down[0, 0])
+    )(out_grad[0], expert_ids, slot_ids, router_logits[0].T, w_router[0].T, saved_routed[0, 0], w_gate_up[0, 0], w_down[0, 0])
     return prev[None], hgrad[None, None]
 
 

time: 101 us -> 79 us (0.78)
  Pallas kernels: 91.2 us -> 73.1 us
  local copies, waits for them, and re-layouts: 8.37 us -> 5.09 us
    pallas_call x1, Pallas kernels: 91.2 us -> 73.1 us  [on_device(): pl.pallas_call(body, out_shape=(jax.ShapeDtypeStruct((TOK, D), BF16), jax...]
    unnamed x4 -> x2, local copies, waits for them, and re-layouts: 8.37 us -> 5.09 us
where the time goes in v2:
time: 79 us; the launch traced here: 78.8 us
  Pallas kernels  73.1 us (93%)
  local copies, waits for them, and re-layouts  5.09 us (6%)
    pallas_call x1, Pallas kernels, on_device(): pl.pallas_call(body, out_shape=(jax.ShapeDtypeStruct((TOK, D), BF16), jax...  73.1 us
    unnamed x2, local copies, waits for them, and re-layouts  5.09 us

profile of v2, /device:TPU:64, one launch (start us, length us, event | category | flops | bytes accessed | tf_op | source)
XLA Modules:
  0.0 78.8 jit_solution(2577075877721094705)
XLA Ops:
  0.6 73.1 %shard_map.95 = (bf16[128,2560]{1,0:T(8,128)(2,1)}, bf16[1056,1024]{1,0:T(8,128)(2,1)}) custom-call(bf16[128,2560]{1,0:T(8,128)(2,1)} %bitcast.17, s32[1,128]{1,0:T(1,128)} %refs_1_.1, s32[1,128]{1,0:T(1,128)} %refs_2_.1, f32[4,128]{1,0:T(4,128)} %bitcast.19, bf16[4,2560]{1,0:T(4,128)(2,1)} %bitcast.18, bf16[1056,1024]{1,0:T(8,128)(2,1)} %bitcast.16, ...), custom_call_target="tpu_custom_call" | custom-call | flops 8999999488 | bytes 14000000 | tf_op jit(solution)/shard_map/pallas_call | solution.py:403
  73.7 2.0 %copy.12 = bf16[1,128,2560]{2,1,0:T(8,128)(2,1)} copy(bf16[1,128,2560]{2,1,0:T(8,128)(2,1)} %bitcast.13) | data formatting | bytes 1310720
  75.7 3.1 %copy.13 = bf16[1,1,1056,1024]{3,2,1,0:T(8,128)(2,1)} copy(bf16[1,1,1056,1024]{3,2,1,0:T(8,128)(2,1)} %bitcast.12) | data formatting | bytes 4325376

commit v3 on v2

v3 whole, which is shorter than its diff:
```python
import jax
import jax.numpy as jnp
from jax import lax
from jax.experimental import pallas as pl
from jax.experimental.pallas import tpu as pltpu
from jax.sharding import PartitionSpec as P

F32, BF16, I32 = jnp.float32, jnp.bfloat16, jnp.int32
SIDE = 4
TOK = 128
MOST = 33
REG = 32
D = 2560
FF_DEV = 512
SLOTS = 1056
QUART = D // 4
TILE_W = QUART + 128
HALF = D // 2
PART = 528

ORDER = [
    (0, 0), (0, 1), (1, 3), (1, 0), (3, 0), (0, 2), (2, 0), (3, 1), (2, 1), (2, 3), (1, 2), (0, 3), (3, 3), (1, 1),
    (3, 2), (2, 2),
]
SLOT = {chunk: i for i, chunk in enumerate(ORDER)}
PLAN = [
    ("x", 1), ("x", 3), ("y+", 0), ("y-", 0), ("e", 1), ("sib", 0, 0), ("e", 3), ("e", 2), ("x", 2), ("prep",),
    ("sib", 0, 3), ("y+", 1), ("y-", 3), ("E0",), ("ea", 2), ("ea", 1), ("yr", 0), ("ea", 3), ("es", 0), ("y-", 2),
    ("sib", 0, 1), ("yr", 1), ("sib", 3, 1), ("y+", 3), ("sib", 1, 0), ("sib", 0, 2), ("yr", 3), ("es", 2), ("es", 3),
    ("y+", 2), ("es", 1), ("sib", 1, 3), ("sib", 3, 0), ("y-", 1), ("step", 0), ("step", 1), ("sib", 2, 0), ("yr", 2),
    ("sib", 1, 2), ("step", 2), ("ext",), ("sib", 2, 1), ("sib", 2, 3), ("step", 3), ("step", 4), ("sib", 1, 1),
    ("fin", 3), ("d-", 1, 0), ("rr", 0), ("sib", 3, 3), ("step", 5), ("fin", 2), ("d-", 1, 1), ("fin", 4), ("rr", 1),
    ("rr", 3), ("fin", 1), ("sib", 3, 2), ("sib", 2, 2), ("step", 6), ("step", 7), ("rs",), ("rt", 2), ("rt", 1),
    ("rt", 3), ("d-", 0, 1), ("fin", 6), ("fin", 0), ("d+", 0, 1), ("fin", 7), ("d+", 1, 0), ("rr", 2), ("d+", 1, 1),
    ("terms",), ("d-", 0, 0), ("ft",), ("d+", 0, 0), ("final", 0, 1), ("d+", 3, 1), ("d-", 3, 1), ("d-", 3, 0),
    ("d+", 3, 0), ("final", 1, 0), ("fin", 5), ("final", 1, 1), ("d-", 2, 1), ("final", 0, 0), ("d+", 2, 1),
    ("d-", 2, 0), ("d+", 2, 0), ("final", 3, 1), ("final", 3, 0), ("final", 2, 1), ("final", 2, 0), ("perm",),
    ("out", 1), ("out", 0),
]
STEPS = 8
PLUS = (0, 1)


def packed(values):
    return sum(v << (2 * i) for i, v in enumerate(values))


PACK = [[packed([ORDER[2 * i + j][axis] for i in range(STEPS)]) for j in range(2)] for axis in range(2)]


def dot(a, b):
    return lax.dot_general(a, b, (((1,), (0,)), ((), ())), preferred_element_type=F32)


def iota(shape, axis):
    return lax.broadcasted_iota(I32, shape, axis)


def onehot(mask):
    return jnp.where(mask, F32(1.0), F32(0.0)).astype(BF16)


def to_column(row, rows):
    mask = iota((rows, 128), 0) == iota((rows, 128), 1)
    return jnp.sum(jnp.where(mask, row, jnp.zeros((), row.dtype)), axis=1, keepdims=True)


def to_row(column):
    shape = (column.shape[0], 128)
    mask = iota(shape, 0) == iota(shape, 1)
    return jnp.sum(jnp.where(mask, column, jnp.zeros((), column.dtype)), axis=0, keepdims=True)


def backward(g, score, kept):
    gate_value, up_value = kept[:, :FF_DEV], kept[:, FF_DEV:]
    sigm = jax.nn.sigmoid(gate_value)
    activated = gate_value * sigm
    slope = sigm * (1.0 + gate_value * (1.0 - sigm))
    hidden = (activated * up_value).astype(BF16).astype(F32)
    inner = jnp.sum(hidden * g, axis=1, keepdims=True)
    hidden_grad = score * g
    hg = jnp.concatenate([hidden_grad * up_value * slope, hidden_grad * activated], axis=1).astype(BF16)
    return hg, inner


def kernel(sections, up_hbm, ids_ref, slots_ref, logits_ref, router_ref, kept_hbm, wgu_hbm, wd_hbm,
           fin_hbm, ft_hbm, rt_hbm, hgrad_hbm,
           up_v, kept_v, wgu_v, wd_v, wgut_v, wdt_v, perm_v, kp_v, hgp_v, x_v, xs_v, es_v, ein_v, eall_v, own_v, sbo_v, sbi_v, out_v,
           rel_v, dir_v, rto_v, rti_v, rts2_v, tl_v, inn_v, fino_v, fto_v, rts_v, hg_v,
           send_sem, recv_sem, sb_send, sb_recv, loc_sem):
    sec = lax.axis_index("section")
    me = lax.axis_index("expert")
    c = lax.rem(me, 2)
    y = lax.rem(me // 2, SIDE)
    x = me // (2 * SIDE)

    def dev(dx=0, dy=0, dc=0, dz=0):
        s = lax.rem(sec + dz + sections, sections)
        e = (lax.rem(x + dx + SIDE, SIDE) * SIDE + lax.rem(y + dy + SIDE, SIDE)) * 2 + lax.rem(c + dc, 2)
        return (s, e)

    table = {}
    for d in (1, 3, 2):
        table["x", d] = (xs_v.at[d - 1], x_v.at[SLOT[0, d], 0], dev(dx=-d))
        table["e", d] = (es_v.at[d], ein_v.at[d - 1], dev(dx=-d))
    for d in range(4):
        n0 = SLOT[0, d]
        table["y+", d] = (x_v.at[n0, 0], x_v.at[SLOT[3, d], 0], dev(dy=1))
        table["y-", d] = (x_v.at[n0, 0], x_v.at[SLOT[1, d], 0], dev(dy=-1))
        if d in PLUS:
            table["yr", d] = (x_v.at[SLOT[3, d], 0], x_v.at[SLOT[2, d], 0], dev(dy=1))
            table["rr", d] = (out_v.at[SLOT[2, d]], rel_v.at[d], dev(dy=1))
        else:
            table["yr", d] = (x_v.at[SLOT[1, d], 0], x_v.at[SLOT[2, d], 0], dev(dy=-1))
            table["rr", d] = (out_v.at[SLOT[2, d]], rel_v.at[d], dev(dy=-1))
        for k in range(4):
            n = SLOT[k, d]
            table["sib", k, d] = (x_v.at[n, 0], x_v.at[n, 1], dev(dc=1))
        for h in range(2):
            table["d+", d, h] = (out_v.at[SLOT[1, d], h], dir_v.at[0, d, h], dev(dy=1))
            table["d-", d, h] = (out_v.at[SLOT[3, d], h], dir_v.at[1, d, h], dev(dy=-1))
            table["f", d, h] = (fino_v.at[d, h], fin_hbm.at[h, d], dev(dx=d, dz=-1))
        table["ft", d] = (fto_v, ft_hbm.at[d], dev(dx=d, dz=-1))
    for k in range(4):
        table["es", k] = (eall_v.at[2 * k], eall_v.at[2 * k + 1], dev(dc=1))
        if k:
            table["ea", k] = (eall_v.at[0], eall_v.at[2 * ((4 - k) % 4)], dev(dy=k))
            table["rt", k] = (rto_v.at[0, k], rti_v.at[(4 - k) % 4], dev(dy=k))
    table[("rs",)] = (rto_v.at[1], rts2_v, dev(dc=1))
    table[("ids",)] = (rts_v, rt_hbm, dev(dz=-1))
    number = {name: i for i, name in enumerate(table)}

    def copy(*name):
        src, dst, device = table[name]
        i = number[name]
        return pltpu.make_async_remote_copy(
            src_ref=src, dst_ref=dst, send_sem=send_sem.at[i], recv_sem=recv_sem.at[i],
            device_id=device, device_id_type=pl.DeviceIdType.MESH)

    def start(*name):
        copy(*name).start()

    def recv(*name):
        copy(*name).wait_recv()

    got = set()

    def need(*name):
        if name not in got:
            recv(*name)
        got.add(name)

    up_copy = pltpu.make_async_copy(up_hbm, up_v, loc_sem.at[4])
    kept_copy = pltpu.make_async_copy(kept_hbm, kept_v, loc_sem.at[0])
    wd_copy = pltpu.make_async_copy(wd_hbm, wd_v, loc_sem.at[1])
    wgu_copy = pltpu.make_async_copy(wgu_hbm, wgu_v, loc_sem.at[2])
    up_copy.start()
    barrier = pltpu.get_barrier_semaphore()
    partners = [dev(dx=d) for d in (1, 2, 3)]
    partners += [dev(dy=k, dc=s) for k in range(4) for s in range(2) if k or s]
    partners += [dev(dx=d, dz=dz) for d in range(4) for dz in (-1, 1)]
    for partner in partners:
        pl.semaphore_signal(barrier, inc=1, device_id=partner, device_id_type=pl.DeviceIdType.MESH)

    wd_copy.start()
    kept_copy.start()
    wgu_copy.start()
    ids_row, slot_row = ids_ref[...], slots_ref[...]
    rel_row = jnp.bitwise_and(x + SIDE - ids_row, 3)
    key = jnp.where(slot_row < REG, rel_row * REG + slot_row, -1)
    perm = onehot(iota((TOK, TOK), 0) == key)
    up_copy.wait()
    up = up_v[...]
    rows = dot(perm, up).astype(BF16)
    x_v[SLOT[0, 0], 0] = rows[:REG]
    for d in range(1, 4):
        xs_v[d - 1] = rows[d * REG:(d + 1) * REG]
    ids_col, slot_col = to_column(ids_row, TOK), to_column(slot_row, TOK)
    chosen = jnp.sum(jnp.where(iota((SIDE, TOK), 0) == ids_row, logits_ref[...], 0.0), axis=0, keepdims=True)
    part = to_column(jax.nn.sigmoid(chosen), TOK)
    fold = jnp.zeros((4 * 16, QUART), F32)
    gates = jnp.zeros((4 * 16, 128), F32)
    for q in range(4):
        place = iota((4 * 16, TOK), 0) == rel_row * 17 + 4 * q
        fold += dot(onehot(place & (slot_row == REG)), up[:, q * QUART:(q + 1) * QUART])
        if q < 3:
            rounded = part.astype(BF16).astype(F32)
            spread = jnp.where(iota((TOK, 128), 1) == slot_col, rounded, 0.0).astype(BF16)
            gates += dot(onehot(place), spread)
            part = part - rounded
    tiles = jnp.concatenate([fold, gates], axis=1).astype(BF16)
    for d in range(4):
        es_v[d] = tiles[16 * d:16 * (d + 1)]
    rts_v[...] = jnp.concatenate([ids_row, slot_row, jnp.zeros((6, TOK), I32)], axis=0)

    def capacity(p):
        return jnp.where(p < 16 * REG, p // REG * MOST + jnp.bitwise_and(p, REG - 1), (p - 16 * REG) * MOST + REG)

    perm_v[...] = onehot(capacity(iota((PART, PART), 0)) == iota((PART, PART), 1))
    inn_v[...] = jnp.zeros_like(inn_v)
    pl.semaphore_wait(barrier, len(partners))
    def fold_tiles():
        for d in (1, 2, 3):
            need("e", d)
        tile = es_v[0].astype(F32)
        for d in (1, 2, 3):
            tile += ein_v[d - 1].astype(F32)
        eall_v[0] = tile.astype(BF16)

    def prepare():
        wd_copy.wait()
        for t in range(5):
            wdt_v[512 * t:512 * (t + 1), :] = wd_v[:, 512 * t:512 * (t + 1)].T
        kept_copy.wait()
        for p in range(2):
            for t in range(2):
                cols = slice(512 * t, 512 * (t + 1))
                kp_v[p, :, cols] = dot(perm_v[...], kept_v[PART * p:PART * (p + 1), cols]).astype(BF16)
        perm_v[...] = onehot(capacity(iota((PART, PART), 1)) == iota((PART, PART), 0))
        wgu_copy.wait()
        for t in range(5):
            wgut_v[:, 512 * t:512 * (t + 1)] = wgu_v[512 * t:512 * (t + 1), :].T

    def need_chunk(k, d):
        if k or d:
            need(*{0: ("x", d), 1: ("y-", d), 2: ("yr", d), 3: ("y+", d)}[k])

    def need_tiles(k):
        need("es", k)
        if k:
            need("ea", (4 - k) % 4)

    def half_copy(n):
        return pltpu.make_async_remote_copy(
            src_ref=sbo_v.at[n], dst_ref=sbi_v.at[n], send_sem=sb_send.at[n], recv_sem=sb_recv.at[n],
            device_id=dev(dc=1), device_id_type=pl.DeviceIdType.MESH)

    def finish(m):
        for j in range(2):
            n = 2 * m + j
            half_copy(n).wait_recv()
            both = own_v[n] + sbi_v[n].astype(F32)
            own_v[n] = both
            out_v[n] = both.astype(BF16)

    def select(q, flip):
        shape = (128, 32) if flip else (32, 128)
        b, place = iota(shape, 1 if flip else 0), iota(shape, 0 if flip else 1)
        idx = 2 * jnp.bitwise_and(b // 2 - y + SIDE, 3) + jnp.bitwise_and(b + c, 1)
        return onehot(place == idx * 16 + 4 * q + jnp.bitwise_and(b // 8 - x + SIDE, 3))

    def extras():
        for k in range(4):
            need_tiles(k)
        spread_tiles = eall_v[...].reshape(8 * 16, TILE_W)
        extra = jnp.concatenate([dot(select(q, False), spread_tiles[:, :QUART]).astype(BF16) for q in range(4)], axis=1)
        gate_rows = dot(select(0, False), spread_tiles[:, QUART:])
        score = jnp.sum(jnp.where(iota((32, 128), 1) == REG, gate_rows, 0.0), axis=1, keepdims=True)
        kept = kp_v[:, 16 * REG:, :].reshape(32, 2 * FF_DEV).astype(F32)
        hg, inner = backward(dot(extra, wdt_v[...]), score, kept)
        hgp_v[:, 16 * REG:, :] = hg.reshape(2, 16, 2 * FF_DEV)
        dx = dot(hg, wgut_v[...]).astype(BF16)
        folded = jnp.zeros((8 * 16, QUART), F32)
        for q in range(4):
            folded += dot(select(q, True), dx[:, q * QUART:(q + 1) * QUART])
        inner_at = jnp.where(iota((32, 128), 1) == REG, inner, 0.0).astype(BF16)
        tl_v[...] = jnp.concatenate([folded, dot(select(0, True), inner_at)], axis=1).astype(BF16)

    def tiles_back():
        inners = inn_v[...].reshape(8 * 16, 128) + tl_v[:, QUART:].astype(F32)
        tiles = jnp.concatenate([tl_v[:, :QUART], inners.astype(BF16)], axis=1).reshape(4, 2, 16, TILE_W)
        rto_v[0] = tiles[:, 0]
        rto_v[1] = tiles[:, 1]

    def add_tiles():
        if ("rs",) not in got:
            need("rs")
            rto_v[0] = (rto_v[0].astype(F32) + rts2_v[...].astype(F32)).astype(BF16)

    def restore():
        for p in range(2):
            for t in range(2):
                cols = slice(512 * t, 512 * (t + 1))
                kept_v[PART * p:PART * (p + 1), cols] = dot(perm_v[...], hgp_v[p, :, cols]).astype(BF16)
        hgrad_copy.start()

    hgrad_copy = pltpu.make_async_copy(kept_v, hgrad_hbm, loc_sem.at[3])
    w_row = jnp.sum(jnp.where(iota((SIDE, D), 0) == x, router_ref[...].astype(F32), 0.0), axis=0, keepdims=True)
    terms = []

    def totals():
        add_tiles()
        for k in (1, 2, 3):
            need("rt", k)
        total = rto_v[0, 0].astype(F32)
        for k in (1, 2, 3):
            total += rti_v[k].astype(F32)
        gate_tile = eall_v[0, :, QUART:].astype(F32)
        kind = jnp.bitwise_and(iota((16, 128), 0), 3)
        all_terms = jnp.zeros((16, 128), F32)
        for d in range(4):
            gate = jnp.sum(jnp.where(kind == d, gate_tile, 0.0), axis=0, keepdims=True)
            inner_row = jnp.sum(jnp.where(iota((16, 128), 0) == d, total[:, QUART:], 0.0), axis=0, keepdims=True)
            terms.append(gate * (1.0 - gate) * inner_row)
            all_terms = jnp.where(kind == d, terms[d], all_terms)
        last_term = jnp.sum(jnp.where(iota((16, 128), 1) == REG, all_terms, 0.0), axis=1, keepdims=True)
        w_fold = jnp.zeros((16, QUART), F32)
        for q in range(4):
            w_fold = jnp.where(iota((16, QUART), 0) // 4 == q, w_row[:, q * QUART:(q + 1) * QUART], w_fold)
        fto_v[...] = (total[:, :QUART] + last_term * w_fold).astype(BF16)

    def final(d, h):
        need("d+", d, h)
        need("d-", d, h)
        n = SLOT[0, d]
        rows = own_v[n, h] + dir_v[0, d, h].astype(F32) + dir_v[1, d, h].astype(F32)
        fino_v[d, h] = (rows + to_column(terms[d], REG) * w_row[:, HALF * h:HALF * (h + 1)]).astype(BF16)
        start("f", d, h)

    def act(kind, *at):
        if kind in ("y+", "y-") and at[0]:
            need("x", *at)
        elif kind == "yr":
            need("y+" if at[0] in PLUS else "y-", *at)
        elif kind == "sib":
            need_chunk(*at)
        elif kind == "es" and at[0]:
            need("ea", (4 - at[0]) % 4)
        elif kind in ("d+", "d-"):
            d, h = at
            if (d in PLUS) == (kind == "d+"):
                need("rr", d)
                n = SLOT[1 if kind == "d+" else 3, d]
                out_v[n, h] = (own_v[n, h] + rel_v[d, h].astype(F32)).astype(BF16)
        elif kind == "rs":
            tiles_back()
        elif kind == "rt":
            add_tiles()
        whole = {"E0": fold_tiles, "prep": prepare, "fin": finish, "ext": extras, "terms": totals, "final": final, "perm": restore}
        if kind in whole:
            whole[kind](*at)
        elif kind == "ft":
            for d in range(4):
                start("ft", d)
        else:
            start(kind, *at)

    parts = [[]]
    for entry in PLAN:
        if entry[0] == "out":
            continue
        if entry[0] == "step":
            parts.append([])
        else:
            parts[-1].append(entry)

    def before(i):
        for entry in parts[i]:
            act(*entry)
        for k, d in ORDER[2 * i:2 * i + 2]:
            need_chunk(k, d)
            need("sib", k, d)
            need_tiles(k)

    start("ids")
    before(0)

    @pl.loop(0, STEPS)
    def _(it):
        for i in range(1, STEPS):
            @pl.when(it == i)
            def _():
                before(i)

        rows = x_v[pl.ds(2 * it, 2)].reshape(4 * REG, D)
        g = dot(rows, wdt_v[...])
        for j in range(2):
            k, d = [jnp.bitwise_and(jnp.right_shift(jnp.int32(PACK[axis][j]), 2 * it), 3) for axis in range(2)]
            for s in range(2):
                at = (2 * j + s) * REG
                idx = 2 * k + s
                b = jnp.bitwise_and(x + d, 3) * 8 + jnp.bitwise_and(y + k, 3) * 2 + jnp.bitwise_and(c + s, 1)
                window = pl.ds(pl.multiple_of(jnp.bitwise_and(b, 15) * REG, REG), REG)
                kept = kp_v[b // 16, window, :].astype(F32)
                line = iota((16, 128), 0) == d
                score_row = jnp.sum(jnp.where(line, eall_v[idx, :, QUART:].astype(F32), 0.0), axis=0, keepdims=True)
                hg, inner = backward(g[at:at + REG], to_column(score_row, REG), kept)
                hg_v[at:at + REG, :] = hg
                inn_v[idx] = jnp.where(line, to_row(inner), inn_v[idx])
                hgp_v[b // 16, window, :] = hg
        for h in range(2):
            dx = dot(hg_v[...], wgut_v[:, HALF * h:HALF * (h + 1)])
            for j in range(2):
                own_v[2 * it + j, h] = dx[2 * j * REG:(2 * j + 1) * REG]
                sbo_v[2 * it + j, h] = dx[(2 * j + 1) * REG:(2 * j + 2) * REG].astype(BF16)
        for j in range(2):
            half_copy(2 * it + j).start()

    for entry in parts[STEPS]:
        act(*entry)

    need("ids")
    for d in range(4):
        need("ft", d)
        for h in range(2):
            need("f", d, h)
    for name in table:
        copy(*name).wait_send()
    for n in range(2 * STEPS):
        half_copy(n).wait_send()
    hgrad_copy.wait()


def assemble(sections, fin_hbm, ft_hbm, rt_hbm, hg_hbm, prev_hbm, hgrad_hbm, fin_v, ft_v, rt_v, hg_v, prev_v, sem):
    x = lax.axis_index("expert") // (2 * SIDE)
    live = lax.axis_index("section") < sections - 1
    into = [pltpu.make_async_copy(a, b, sem.at[i]) for i, (a, b) in enumerate(
        ((rt_hbm, rt_v), (ft_hbm, ft_v), (fin_hbm.at[0], fin_v.at[0]), (fin_hbm.at[1], fin_v.at[1])))]
    span = SLOTS // 3
    part = [pl.ds(span * i, span) for i in range(3)]
    hg_in = [pltpu.make_async_copy(hg_hbm.at[p], hg_v.at[p], sem.at[4 + i]) for i, p in enumerate(part)]
    hg_out = [pltpu.make_async_copy(hg_v.at[p], hgrad_hbm.at[p], sem.at[7 + i]) for i, p in enumerate(part)]
    prev_out = [pltpu.make_async_copy(prev_v.at[h], prev_hbm.at[:, pl.ds(h * HALF, HALF)], sem.at[10 + h]) for h in range(2)]
    for copy in into + hg_in:
        copy.start()
    for copy in into[:2]:
        copy.wait()
    ids_col, slot_col = to_column(rt_v[0:1, :], TOK), to_column(rt_v[1:2, :], TOK)
    rel_col = jnp.bitwise_and(x + SIDE - ids_col, 3)
    back = onehot((iota((TOK, TOK), 1) == jnp.where(slot_col < REG, rel_col * REG + slot_col, -1)) & live)
    fts = ft_v[...].reshape(4 * 16, QUART)
    for h in range(2):
        into[2 + h].wait()
        whole = dot(back, fin_v[h].reshape(TOK, HALF))
        extra = []
        for q in (2 * h, 2 * h + 1):
            pick = onehot((iota((TOK, 4 * 16), 1) == jnp.where(slot_col == REG, rel_col * 17 + 4 * q, -1)) & live)
            extra.append(dot(pick, fts))
        prev_v[h] = (whole + jnp.concatenate(extra, axis=1)).astype(BF16)
        prev_out[h].start()
        hg_in[h].wait()
        hg_out[h].start()
    hg_in[2].wait()
    hg_out[2].start()
    for copy in prev_out + hg_out:
        copy.wait()


def on_device(out_grad, expert_ids, slot_ids, router_logits, saved_routed, w_gate_up, w_down, w_router):
    sections = lax.axis_size("section")
    vmem = pl.BlockSpec(memory_space=pltpu.VMEM)
    hbm = pl.BlockSpec(memory_space=pl.ANY)

    def body(*refs):
        kernel(sections, *refs)

    count = 96
    fin, ft, rt, hg = pl.pallas_call(
        body,
        out_shape=(
            jax.ShapeDtypeStruct((2, 4, REG, HALF), BF16),
            jax.ShapeDtypeStruct((4, 16, QUART), BF16),
            jax.ShapeDtypeStruct((8, TOK), I32),
            jax.ShapeDtypeStruct((SLOTS, 2 * FF_DEV), BF16),
        ),
        in_specs=[hbm] + [vmem] * 4 + [hbm] * 3,
        out_specs=(hbm,) * 4,
        scratch_shapes=[
            pltpu.VMEM((TOK, D), BF16),
            pltpu.VMEM((SLOTS, 2 * FF_DEV), BF16),
            pltpu.VMEM((D, 2 * FF_DEV), BF16),
            pltpu.VMEM((FF_DEV, D), BF16),
            pltpu.VMEM((2 * FF_DEV, D), BF16),
            pltpu.VMEM((D, FF_DEV), BF16),
            pltpu.VMEM((PART, PART), BF16),
            pltpu.VMEM((2, PART, 2 * FF_DEV), BF16),
            pltpu.VMEM((2, PART, 2 * FF_DEV), BF16),
            pltpu.VMEM((16, 2, REG, D), BF16),
            pltpu.VMEM((3, REG, D), BF16),
            pltpu.VMEM((4, 16, TILE_W), BF16),
            pltpu.VMEM((3, 16, TILE_W), BF16),
            pltpu.VMEM((8, 16, TILE_W), BF16),
            pltpu.VMEM((16, 2, REG, HALF), F32),
            pltpu.VMEM((16, 2, REG, HALF), BF16),
            pltpu.VMEM((16, 2, REG, HALF), BF16),
            pltpu.VMEM((16, 2, REG, HALF), BF16),
            pltpu.VMEM((4, 2, REG, HALF), BF16),
            pltpu.VMEM((2, 4, 2, REG, HALF), BF16),
            pltpu.VMEM((2, 4, 16, TILE_W), BF16),
            pltpu.VMEM((4, 16, TILE_W), BF16),
            pltpu.VMEM((4, 16, TILE_W), BF16),
            pltpu.VMEM((8 * 16, TILE_W), BF16),
            pltpu.VMEM((8, 16, 128), F32),
            pltpu.VMEM((4, 2, REG, HALF), BF16),
            pltpu.VMEM((16, QUART), BF16),
            pltpu.VMEM((8, TOK), I32),
            pltpu.VMEM((4 * REG, 2 * FF_DEV), BF16),
            pltpu.SemaphoreType.DMA((count,)),
            pltpu.SemaphoreType.DMA((count,)),
            pltpu.SemaphoreType.DMA((16,)),
            pltpu.SemaphoreType.DMA((16,)),
            pltpu.SemaphoreType.DMA((5,)),
        ],
        compiler_params=pltpu.CompilerParams(collective_id=0, has_side_effects=True, vmem_limit_bytes=60 * 2**20),
        cost_estimate=pl.CostEstimate(flops=9 * 10**9, bytes_accessed=14 * 10**6, transcendentals=600000),
    )(out_grad[0], expert_ids, slot_ids, router_logits[0].T, w_router[0].T, saved_routed[0, 0], w_gate_up[0, 0], w_down[0, 0])

    def last(*refs):
        assemble(sections, *refs)

    prev, hgrad = pl.pallas_call(
        last,
        out_shape=(jax.ShapeDtypeStruct((TOK, D), BF16), jax.ShapeDtypeStruct((SLOTS, 2 * FF_DEV), BF16)),
        in_specs=[hbm] * 4,
        out_specs=(hbm, hbm),
        scratch_shapes=[
            pltpu.VMEM((2, 4, REG, HALF), BF16),
            pltpu.VMEM((4, 16, QUART), BF16),
            pltpu.VMEM((8, TOK), I32),
            pltpu.VMEM((SLOTS, 2 * FF_DEV), BF16),
            pltpu.VMEM((2, TOK, HALF), BF16),
            pltpu.SemaphoreType.DMA((12,)),
        ],
        compiler_params=pltpu.CompilerParams(vmem_limit_bytes=60 * 2**20),
        cost_estimate=pl.CostEstimate(flops=10**8, bytes_accessed=6 * 10**6, transcendentals=0),
    )(fin, ft, rt, hg)
    return prev[None], hgrad[None, None]


def solution(mesh):
    placed = (
        P("section", "expert", None),
        P("section", "expert"),
        P("section", "expert"),
        P("section", "expert", None),
        P("section", "expert", None, None),
        P("section", "expert", None, None),
        P("section", "expert", None, None),
        P("section", None, None),
    )
    return jax.shard_map(
        on_device,
        mesh=mesh,
        in_specs=placed,
        out_specs=(P("section", "expert", None), P("section", "expert", None, None)),
        check_vma=False,
    )
```

time: 79 us -> 67.7 us (0.86)
  Pallas kernels: 73.1 us -> 66.8 us
  local copies, waits for them, and re-layouts: 5.09 us -> 0 us
    pallas_call x1 -> x2, Pallas kernels: 73.1 us -> 66.8 us  [the longest x1 63.8 us: on_device(): pl.pallas_call(body, out_shape=(jax.ShapeDtypeStruct((2, 4, REG, HALF), B...]
    unnamed x2 -> x0, local copies, waits for them, and re-layouts: 5.09 us -> none
where the time goes in v3:
time: 67.7 us; the launch traced here: 67.4 us
  Pallas kernels  66.8 us (99%)
    pallas_call x1, Pallas kernels, on_device(): pl.pallas_call(body, out_shape=(jax.ShapeDtypeStruct((2, 4, REG, HALF), B...  63.8 us
    pallas_call x1, Pallas kernels, on_device(): pl.pallas_call(last, out_shape=(jax.ShapeDtypeStruct((TOK, D), BF16), jax...  3.01 us

profile of v3, /device:TPU:64, one launch (start us, length us, event | category | flops | bytes accessed | tf_op | source)
XLA Modules:
  0.0 67.4 jit_solution(14869572278430846692)
XLA Ops:
  0.6 63.8 %shard_map.95 = (bf16[2,4,32,1280]{3,2,1,0:T(8,128)(2,1)}, bf16[4,16,640]{2,1,0:T(8,128)(2,1)}, s32[8,128]{1,0:T(8,128)}, bf16[1056,1024]{1,0:T(8,128)(2,1)}) custom-call(bf16[128,2560]{1,0:T(8,128)(2,1)} %bitcast.16, s32[1,128]{1,0:T(1,128)} %refs_1_.1, s32[1,128]{1,0:T(1,128)} %refs_2_.1, f32[4,128]{1,0:T(4,128)} %bitcast.19, bf16[4,2560]{1,0:T(4,128)(2,1)} %bitcast.18, ...), custom_call_target="tpu_custom_call" | custom-call | flops 8999999488 | bytes 14000000 | tf_op jit(solution)/shard_map/pallas_call | solution.py:458
  64.4 3.0 %shard_map.96 = (bf16[128,2560]{1,0:T(8,128)(2,1)}, bf16[1056,1024]{1,0:T(8,128)(2,1)}) custom-call(bf16[2,4,32,1280]{3,2,1,0:T(8,128)(2,1)} %get-tuple-element.8.refs_0_, bf16[4,16,640]{2,1,0:T(8,128)(2,1)} %get-tuple-element.9.refs_1_, s32[8,128]{1,0:T(8,128)} %get-tuple-element.10.refs_2_, bf16[1056,1024]{1,0:T(8,128)(2,1)} %get-tuple-element.11.refs_3_), custom_call_target="tpu_custom_call" | custom-call | flops 100000000 | bytes 6000000 | tf_op jit(solution)/shard_map/pallas_call | solution.py:511

commit v4 on v3

--- a/solution.py
+++ b/solution.py
@@ -19,23 +19,24 @@
 PART = 528
 
 ORDER = [
-    (0, 0), (0, 1), (1, 3), (1, 0), (3, 0), (0, 2), (2, 0), (3, 1), (2, 1), (2, 3), (1, 2), (0, 3), (3, 3), (1, 1),
-    (3, 2), (2, 2),
+    (3, 0), (3, 1), (0, 1), (2, 0), (1, 3), (1, 0), (2, 3), (2, 1), (1, 2), (0, 0), (0, 2), (0, 3), (3, 2), (1, 1),
+    (2, 2), (3, 3),
 ]
 SLOT = {chunk: i for i, chunk in enumerate(ORDER)}
 PLAN = [
-    ("x", 1), ("x", 3), ("y+", 0), ("y-", 0), ("e", 1), ("sib", 0, 0), ("e", 3), ("e", 2), ("x", 2), ("prep",),
-    ("sib", 0, 3), ("y+", 1), ("y-", 3), ("E0",), ("ea", 2), ("ea", 1), ("yr", 0), ("ea", 3), ("es", 0), ("y-", 2),
-    ("sib", 0, 1), ("yr", 1), ("sib", 3, 1), ("y+", 3), ("sib", 1, 0), ("sib", 0, 2), ("yr", 3), ("es", 2), ("es", 3),
-    ("y+", 2), ("es", 1), ("sib", 1, 3), ("sib", 3, 0), ("y-", 1), ("step", 0), ("step", 1), ("sib", 2, 0), ("yr", 2),
-    ("sib", 1, 2), ("step", 2), ("ext",), ("sib", 2, 1), ("sib", 2, 3), ("step", 3), ("step", 4), ("sib", 1, 1),
-    ("fin", 3), ("d-", 1, 0), ("rr", 0), ("sib", 3, 3), ("step", 5), ("fin", 2), ("d-", 1, 1), ("fin", 4), ("rr", 1),
-    ("rr", 3), ("fin", 1), ("sib", 3, 2), ("sib", 2, 2), ("step", 6), ("step", 7), ("rs",), ("rt", 2), ("rt", 1),
-    ("rt", 3), ("d-", 0, 1), ("fin", 6), ("fin", 0), ("d+", 0, 1), ("fin", 7), ("d+", 1, 0), ("rr", 2), ("d+", 1, 1),
-    ("terms",), ("d-", 0, 0), ("ft",), ("d+", 0, 0), ("final", 0, 1), ("d+", 3, 1), ("d-", 3, 1), ("d-", 3, 0),
-    ("d+", 3, 0), ("final", 1, 0), ("fin", 5), ("final", 1, 1), ("d-", 2, 1), ("final", 0, 0), ("d+", 2, 1),
-    ("d-", 2, 0), ("d+", 2, 0), ("final", 3, 1), ("final", 3, 0), ("final", 2, 1), ("final", 2, 0), ("perm",),
-    ("out", 1), ("out", 0),
+    ("x", 3, 0), ("x", 1, 1), ("y+", 0, 0), ("y-", 0, 0), ("x", 1, 0), ("y+", 0, 1), ("x", 3, 1), ("y-", 0, 1),
+    ("e", 2), ("prep",), ("y-", 3, 0), ("y+", 1, 1), ("e", 3), ("e", 1), ("x", 2, 1), ("sib", 0, 3), ("y+", 1, 0),
+    ("y-", 3, 1), ("sib", 3, 0), ("E0",), ("y-", 1, 1), ("ea", 1), ("es", 0), ("ea", 3), ("ea", 2), ("yr", 0),
+    ("x", 2, 0), ("sib", 3, 1), ("sib", 1, 0), ("yr", 3), ("y-", 2, 1), ("yr", 1), ("sib", 1, 3), ("y+", 2, 1),
+    ("es", 3), ("step", 0), ("y+", 3, 1), ("es", 2), ("y+", 2, 0), ("y+", 3, 0), ("sib", 0, 0), ("y-", 2, 0), ("es", 1),
+    ("y-", 1, 0), ("sib", 0, 2), ("sib", 2, 0), ("sib", 0, 1), ("fin", 0), ("ext",), ("step", 1), ("sib", 2, 3),
+    ("sib", 2, 1), ("step", 2), ("yr", 2), ("sib", 1, 2), ("step", 3), ("step", 4), ("fin", 3), ("rr", 3), ("rr", 1),
+    ("sib", 3, 2), ("d-", 1, 1), ("d-", 1, 0), ("sib", 1, 1), ("step", 5), ("fin", 1), ("rr", 0), ("sib", 2, 2),
+    ("sib", 3, 3), ("step", 6), ("step", 7), ("rs",), ("fin", 5), ("rt", 2), ("rt", 3), ("rt", 1), ("fin", 4),
+    ("fin", 7), ("d-", 3, 0), ("rr", 2), ("fin", 6), ("fin", 2), ("d-", 3, 1), ("d+", 3, 0), ("d-", 0, 1), ("d+", 1, 1),
+    ("d+", 1, 0), ("terms",), ("ft",), ("d+", 3, 1), ("d+", 0, 1), ("final", 3, 0), ("d+", 2, 0), ("final", 1, 1),
+    ("final", 1, 0), ("d-", 2, 0), ("final", 3, 1), ("d+", 2, 1), ("d-", 2, 1), ("final", 0, 1), ("d-", 0, 0),
+    ("d+", 0, 0), ("final", 2, 0), ("perm",), ("final", 2, 1), ("final", 0, 0),
 ]
 STEPS = 8
 PLUS = (0, 1)
@@ -101,12 +102,16 @@
 
     table = {}
     for d in (1, 3, 2):
-        table["x", d] = (xs_v.at[d - 1], x_v.at[SLOT[0, d], 0], dev(dx=-d))
+        for part in range(2):
+            half = pl.ds(16 * part, 16)
+            table["x", d, part] = (xs_v.at[d - 1, half], x_v.at[SLOT[0, d], 0, half], dev(dx=-d))
         table["e", d] = (es_v.at[d], ein_v.at[d - 1], dev(dx=-d))
     for d in range(4):
         n0 = SLOT[0, d]
-        table["y+", d] = (x_v.at[n0, 0], x_v.at[SLOT[3, d], 0], dev(dy=1))
-        table["y-", d] = (x_v.at[n0, 0], x_v.at[SLOT[1, d], 0], dev(dy=-1))
+        for part in range(2):
+            half = pl.ds(16 * part, 16)
+            table["y+", d, part] = (x_v.at[n0, 0, half], x_v.at[SLOT[3, d], 0, half], dev(dy=1))
+            table["y-", d, part] = (x_v.at[n0, 0, half], x_v.at[SLOT[1, d], 0, half], dev(dy=-1))
         if d in PLUS:
             table["yr", d] = (x_v.at[SLOT[3, d], 0], x_v.at[SLOT[2, d], 0], dev(dy=1))
             table["rr", d] = (out_v.at[SLOT[2, d]], rel_v.at[d], dev(dy=1))
@@ -222,8 +227,11 @@
             wgut_v[:, 512 * t:512 * (t + 1)] = wgu_v[512 * t:512 * (t + 1), :].T
 
     def need_chunk(k, d):
-        if k or d:
-            need(*{0: ("x", d), 1: ("y-", d), 2: ("yr", d), 3: ("y+", d)}[k])
+        if k == 2:
+            need("yr", d)
+        elif k or d:
+            for part in range(2):
+                need({0: "x", 1: "y-", 3: "y+"}[k], d, part)
 
     def need_tiles(k):
         need("es", k)
@@ -321,7 +329,7 @@
         if kind in ("y+", "y-") and at[0]:
             need("x", *at)
         elif kind == "yr":
-            need("y+" if at[0] in PLUS else "y-", *at)
+            need_chunk(3 if at[0] in PLUS else 1, *at)
         elif kind == "sib":
             need_chunk(*at)
         elif kind == "es" and at[0]:
@@ -411,26 +419,20 @@
     hgrad_copy.wait()
 
 
-def assemble(sections, fin_hbm, ft_hbm, rt_hbm, hg_hbm, prev_hbm, hgrad_hbm, fin_v, ft_v, rt_v, hg_v, prev_v, sem):
+def assemble(sections, fin_v, ft_v, rt_v, hg_any, prev_hbm, hgrad_hbm, prev_v, sem):
     x = lax.axis_index("expert") // (2 * SIDE)
     live = lax.axis_index("section") < sections - 1
-    into = [pltpu.make_async_copy(a, b, sem.at[i]) for i, (a, b) in enumerate(
-        ((rt_hbm, rt_v), (ft_hbm, ft_v), (fin_hbm.at[0], fin_v.at[0]), (fin_hbm.at[1], fin_v.at[1])))]
     span = SLOTS // 3
     part = [pl.ds(span * i, span) for i in range(3)]
-    hg_in = [pltpu.make_async_copy(hg_hbm.at[p], hg_v.at[p], sem.at[4 + i]) for i, p in enumerate(part)]
-    hg_out = [pltpu.make_async_copy(hg_v.at[p], hgrad_hbm.at[p], sem.at[7 + i]) for i, p in enumerate(part)]
-    prev_out = [pltpu.make_async_copy(prev_v.at[h], prev_hbm.at[:, pl.ds(h * HALF, HALF)], sem.at[10 + h]) for h in range(2)]
-    for copy in into + hg_in:
+    out = [pltpu.make_async_copy(hg_any.at[p], hgrad_hbm.at[p], sem.at[2 + i]) for i, p in enumerate(part)]
+    prev_out = [pltpu.make_async_copy(prev_v.at[h], prev_hbm.at[:, pl.ds(h * HALF, HALF)], sem.at[h]) for h in range(2)]
+    for copy in out:
         copy.start()
-    for copy in into[:2]:
-        copy.wait()
     ids_col, slot_col = to_column(rt_v[0:1, :], TOK), to_column(rt_v[1:2, :], TOK)
     rel_col = jnp.bitwise_and(x + SIDE - ids_col, 3)
     back = onehot((iota((TOK, TOK), 1) == jnp.where(slot_col < REG, rel_col * REG + slot_col, -1)) & live)
     fts = ft_v[...].reshape(4 * 16, QUART)
     for h in range(2):
-        into[2 + h].wait()
         whole = dot(back, fin_v[h].reshape(TOK, HALF))
         extra = []
         for q in (2 * h, 2 * h + 1):
@@ -438,11 +440,7 @@
             extra.append(dot(pick, fts))
         prev_v[h] = (whole + jnp.concatenate(extra, axis=1)).astype(BF16)
         prev_out[h].start()
-        hg_in[h].wait()
-        hg_out[h].start()
-    hg_in[2].wait()
-    hg_out[2].start()
-    for copy in prev_out + hg_out:
+    for copy in prev_out + out:
         copy.wait()
 
 
@@ -458,10 +456,10 @@
     fin, ft, rt, hg = pl.pallas_call(
         body,
         out_shape=(
-            jax.ShapeDtypeStruct((2, 4, REG, HALF), BF16),
-            jax.ShapeDtypeStruct((4, 16, QUART), BF16),
-            jax.ShapeDtypeStruct((8, TOK), I32),
-            jax.ShapeDtypeStruct((SLOTS, 2 * FF_DEV), BF16),
+            pltpu.VMEM((2, 4, REG, HALF), BF16),
+            pltpu.VMEM((4, 16, QUART), BF16),
+            pltpu.VMEM((8, TOK), I32),
+            pltpu.VMEM((SLOTS, 2 * FF_DEV), BF16),
         ),
         in_specs=[hbm] + [vmem] * 4 + [hbm] * 3,
         out_specs=(hbm,) * 4,
@@ -501,29 +499,26 @@
             pltpu.SemaphoreType.DMA((16,)),
             pltpu.SemaphoreType.DMA((5,)),
         ],
-        compiler_params=pltpu.CompilerParams(collective_id=0, has_side_effects=True, vmem_limit_bytes=60 * 2**20),
+        compiler_params=pltpu.CompilerParams(collective_id=0, has_side_effects=True, vmem_limit_bytes=56 * 2**20),
         cost_estimate=pl.CostEstimate(flops=9 * 10**9, bytes_accessed=14 * 10**6, transcendentals=600000),
     )(out_grad[0], expert_ids, slot_ids, router_logits[0].T, w_router[0].T, saved_routed[0, 0], w_gate_up[0, 0], w_down[0, 0])
 
     def last(*refs):
         assemble(sections, *refs)
 
+    held = [pltpu.with_memory_space_constraint(a, pltpu.VMEM) for a in (fin, ft, rt, hg)]
     prev, hgrad = pl.pallas_call(
         last,
         out_shape=(jax.ShapeDtypeStruct((TOK, D), BF16), jax.ShapeDtypeStruct((SLOTS, 2 * FF_DEV), BF16)),
-        in_specs=[hbm] * 4,
+        in_specs=[vmem] * 3 + [hbm],
         out_specs=(hbm, hbm),
         scratch_shapes=[
-            pltpu.VMEM((2, 4, REG, HALF), BF16),
-            pltpu.VMEM((4, 16, QUART), BF16),
-            pltpu.VMEM((8, TOK), I32),
-            pltpu.VMEM((SLOTS, 2 * FF_DEV), BF16),
             pltpu.VMEM((2, TOK, HALF), BF16),
-            pltpu.SemaphoreType.DMA((12,)),
+            pltpu.SemaphoreType.DMA((5,)),
         ],
-        compiler_params=pltpu.CompilerParams(vmem_limit_bytes=60 * 2**20),
+        compiler_params=pltpu.CompilerParams(vmem_limit_bytes=32 * 2**20),
         cost_estimate=pl.CostEstimate(flops=10**8, bytes_accessed=6 * 10**6, transcendentals=0),
-    )(fin, ft, rt, hg)
+    )(*held)
     return prev[None], hgrad[None, None]
 
 

time: 67.7 us -> 67.7 us (level)
    pallas_call x1, Pallas kernels: 3.01 us -> 1.61 us  [on_device(): pl.pallas_call(last, out_shape=(jax.ShapeDtypeStruct((TOK, D), BF16), jax...]
    pallas_call x1, Pallas kernels: 63.8 us -> 64.8 us  [on_device(): pl.pallas_call(body, out_shape=(pltpu.VMEM((2, 4, REG, HALF), BF16), pltp...]
where the time goes in v4:
time: 67.7 us; the launch traced here: 67 us
  Pallas kernels  66.4 us (98%)
    pallas_call x1, Pallas kernels, on_device(): pl.pallas_call(body, out_shape=(pltpu.VMEM((2, 4, REG, HALF), BF16), pltp...  64.8 us
    pallas_call x1, Pallas kernels, on_device(): pl.pallas_call(last, out_shape=(jax.ShapeDtypeStruct((TOK, D), BF16), jax...  1.61 us

profile of v4, /device:TPU:64, one launch (start us, length us, event | category | flops | bytes accessed | tf_op | source)
XLA Modules:
  0.0 67.0 jit_solution(17128849210653111361)
XLA Ops:
  0.6 64.8 %shard_map.95 = (bf16[2,4,32,1280]{3,2,1,0:T(8,128)(2,1)S(1)}, bf16[4,16,640]{2,1,0:T(8,128)(2,1)S(1)}, s32[8,128]{1,0:T(8,128)S(1)}, bf16[1056,1024]{1,0:T(8,128)(2,1)S(1)}) custom-call(bf16[128,2560]{1,0:T(8,128)(2,1)} %bitcast.16, s32[1,128]{1,0:T(1,128)} %refs_1_.1, s32[1,128]{1,0:T(1,128)} %refs_2_.1, f32[4,128]{1,0:T(4,128)} %bitcast.19, ...), custom_call_target="tpu_custom_call" | custom-call | flops 8999999488 | bytes 14000000 | tf_op jit(solution)/shard_map/pallas_call | solution.py:456
  65.4 1.6 %shard_map.96 = (bf16[128,2560]{1,0:T(8,128)(2,1)}, bf16[1056,1024]{1,0:T(8,128)(2,1)}) custom-call(bf16[2,4,32,1280]{3,2,1,0:T(8,128)(2,1)S(1)} %get-tuple-element.8.refs_0_, bf16[4,16,640]{2,1,0:T(8,128)(2,1)S(1)} %get-tuple-element.9.refs_1_, s32[8,128]{1,0:T(8,128)S(1)} %get-tuple-element.10.refs_2_, bf16[1056,1024]{1,0:T(8,128)(2,1)S(1)} %get-tuple-element.11.refs_3_), custom_call_target="tpu_custom_call" | custom-call | flops 100000000 | bytes 6000000 | tf_op jit(solution)/shard_map/pallas_call | solution.py:510

commit v5 on v4

--- a/solution.py
+++ b/solution.py
@@ -19,24 +19,23 @@
 PART = 528
 
 ORDER = [
-    (3, 0), (3, 1), (0, 1), (2, 0), (1, 3), (1, 0), (2, 3), (2, 1), (1, 2), (0, 0), (0, 2), (0, 3), (3, 2), (1, 1),
-    (2, 2), (3, 3),
+    (0, 0), (0, 1), (1, 3), (1, 0), (3, 0), (0, 2), (2, 0), (3, 1), (2, 1), (2, 3), (1, 2), (0, 3), (3, 3), (1, 1),
+    (3, 2), (2, 2),
 ]
 SLOT = {chunk: i for i, chunk in enumerate(ORDER)}
 PLAN = [
-    ("x", 3, 0), ("x", 1, 1), ("y+", 0, 0), ("y-", 0, 0), ("x", 1, 0), ("y+", 0, 1), ("x", 3, 1), ("y-", 0, 1),
-    ("e", 2), ("prep",), ("y-", 3, 0), ("y+", 1, 1), ("e", 3), ("e", 1), ("x", 2, 1), ("sib", 0, 3), ("y+", 1, 0),
-    ("y-", 3, 1), ("sib", 3, 0), ("E0",), ("y-", 1, 1), ("ea", 1), ("es", 0), ("ea", 3), ("ea", 2), ("yr", 0),
-    ("x", 2, 0), ("sib", 3, 1), ("sib", 1, 0), ("yr", 3), ("y-", 2, 1), ("yr", 1), ("sib", 1, 3), ("y+", 2, 1),
-    ("es", 3), ("step", 0), ("y+", 3, 1), ("es", 2), ("y+", 2, 0), ("y+", 3, 0), ("sib", 0, 0), ("y-", 2, 0), ("es", 1),
-    ("y-", 1, 0), ("sib", 0, 2), ("sib", 2, 0), ("sib", 0, 1), ("fin", 0), ("ext",), ("step", 1), ("sib", 2, 3),
-    ("sib", 2, 1), ("step", 2), ("yr", 2), ("sib", 1, 2), ("step", 3), ("step", 4), ("fin", 3), ("rr", 3), ("rr", 1),
-    ("sib", 3, 2), ("d-", 1, 1), ("d-", 1, 0), ("sib", 1, 1), ("step", 5), ("fin", 1), ("rr", 0), ("sib", 2, 2),
-    ("sib", 3, 3), ("step", 6), ("step", 7), ("rs",), ("fin", 5), ("rt", 2), ("rt", 3), ("rt", 1), ("fin", 4),
-    ("fin", 7), ("d-", 3, 0), ("rr", 2), ("fin", 6), ("fin", 2), ("d-", 3, 1), ("d+", 3, 0), ("d-", 0, 1), ("d+", 1, 1),
-    ("d+", 1, 0), ("terms",), ("ft",), ("d+", 3, 1), ("d+", 0, 1), ("final", 3, 0), ("d+", 2, 0), ("final", 1, 1),
-    ("final", 1, 0), ("d-", 2, 0), ("final", 3, 1), ("d+", 2, 1), ("d-", 2, 1), ("final", 0, 1), ("d-", 0, 0),
-    ("d+", 0, 0), ("final", 2, 0), ("perm",), ("final", 2, 1), ("final", 0, 0),
+    ("x", 1), ("x", 3), ("y+", 0), ("y-", 0), ("e", 1), ("sib", 0, 0), ("e", 3), ("e", 2), ("x", 2), ("prep",),
+    ("sib", 0, 3), ("y+", 1), ("y-", 3), ("E0",), ("ea", 2), ("ea", 1), ("yr", 0), ("ea", 3), ("es", 0), ("y-", 2),
+    ("sib", 0, 1), ("yr", 1), ("sib", 3, 1), ("y+", 3), ("sib", 1, 0), ("sib", 0, 2), ("yr", 3), ("es", 2), ("es", 3),
+    ("y+", 2), ("es", 1), ("sib", 1, 3), ("sib", 3, 0), ("y-", 1), ("step", 0), ("step", 1), ("sib", 2, 0), ("yr", 2),
+    ("sib", 1, 2), ("step", 2), ("ext",), ("sib", 2, 1), ("sib", 2, 3), ("step", 3), ("step", 4), ("sib", 1, 1),
+    ("fin", 3), ("d-", 1, 0), ("rr", 0), ("sib", 3, 3), ("step", 5), ("fin", 2), ("d-", 1, 1), ("fin", 4), ("rr", 1),
+    ("rr", 3), ("fin", 1), ("sib", 3, 2), ("sib", 2, 2), ("step", 6), ("step", 7), ("rs",), ("rt", 2), ("rt", 1),
+    ("rt", 3), ("d-", 0, 1), ("fin", 6), ("fin", 0), ("d+", 0, 1), ("fin", 7), ("d+", 1, 0), ("rr", 2), ("d+", 1, 1),
+    ("terms",), ("d-", 0, 0), ("ft",), ("d+", 0, 0), ("final", 0, 1), ("d+", 3, 1), ("d-", 3, 1), ("d-", 3, 0),
+    ("d+", 3, 0), ("final", 1, 0), ("fin", 5), ("final", 1, 1), ("d-", 2, 1), ("final", 0, 0), ("d+", 2, 1),
+    ("d-", 2, 0), ("d+", 2, 0), ("final", 3, 1), ("final", 3, 0), ("final", 2, 1), ("final", 2, 0), ("perm",),
+    ("out", 1), ("out", 0),
 ]
 STEPS = 8
 PLUS = (0, 1)
@@ -102,16 +101,12 @@
 
     table = {}
     for d in (1, 3, 2):
-        for part in range(2):
-            half = pl.ds(16 * part, 16)
-            table["x", d, part] = (xs_v.at[d - 1, half], x_v.at[SLOT[0, d], 0, half], dev(dx=-d))
+        table["x", d] = (xs_v.at[d - 1], x_v.at[SLOT[0, d], 0], dev(dx=-d))
         table["e", d] = (es_v.at[d], ein_v.at[d - 1], dev(dx=-d))
     for d in range(4):
         n0 = SLOT[0, d]
-        for part in range(2):
-            half = pl.ds(16 * part, 16)
-            table["y+", d, part] = (x_v.at[n0, 0, half], x_v.at[SLOT[3, d], 0, half], dev(dy=1))
-            table["y-", d, part] = (x_v.at[n0, 0, half], x_v.at[SLOT[1, d], 0, half], dev(dy=-1))
+        table["y+", d] = (x_v.at[n0, 0], x_v.at[SLOT[3, d], 0], dev(dy=1))
+        table["y-", d] = (x_v.at[n0, 0], x_v.at[SLOT[1, d], 0], dev(dy=-1))
         if d in PLUS:
             table["yr", d] = (x_v.at[SLOT[3, d], 0], x_v.at[SLOT[2, d], 0], dev(dy=1))
             table["rr", d] = (out_v.at[SLOT[2, d]], rel_v.at[d], dev(dy=1))
@@ -227,11 +222,8 @@
             wgut_v[:, 512 * t:512 * (t + 1)] = wgu_v[512 * t:512 * (t + 1), :].T
 
     def need_chunk(k, d):
-        if k == 2:
-            need("yr", d)
-        elif k or d:
-            for part in range(2):
-                need({0: "x", 1: "y-", 3: "y+"}[k], d, part)
+        if k or d:
+            need({0: "x", 1: "y-", 2: "yr", 3: "y+"}[k], d)
 
     def need_tiles(k):
         need("es", k)

time: 67.7 us -> 66.2 us (0.978)
  Pallas kernels: 66.4 us -> 65.3 us
    pallas_call x1, Pallas kernels: 64.8 us -> 63.7 us  [on_device(): pl.pallas_call(body, out_shape=(pltpu.VMEM((2, 4, REG, HALF), BF16), pltp...]
where the time goes in v5:
time: 66.2 us; the launch traced here: 66 us
  Pallas kernels  65.3 us (99%)
    pallas_call x1, Pallas kernels, on_device(): pl.pallas_call(body, out_shape=(pltpu.VMEM((2, 4, REG, HALF), BF16), pltp...  63.7 us
    pallas_call x1, Pallas kernels, on_device(): pl.pallas_call(last, out_shape=(jax.ShapeDtypeStruct((TOK, D), BF16), jax...  1.61 us

profile of v5, /device:TPU:64, one launch (start us, length us, event | category | flops | bytes accessed | tf_op | source)
XLA Modules:
  0.0 66.0 jit_solution(10773103860200246356)
XLA Ops:
  0.6 63.7 %shard_map.95 = (bf16[2,4,32,1280]{3,2,1,0:T(8,128)(2,1)S(1)}, bf16[4,16,640]{2,1,0:T(8,128)(2,1)S(1)}, s32[8,128]{1,0:T(8,128)S(1)}, bf16[1056,1024]{1,0:T(8,128)(2,1)S(1)}) custom-call(bf16[128,2560]{1,0:T(8,128)(2,1)} %bitcast.16, s32[1,128]{1,0:T(1,128)} %refs_1_.1, s32[1,128]{1,0:T(1,128)} %refs_2_.1, f32[4,128]{1,0:T(4,128)} %bitcast.19, ...), custom_call_target="tpu_custom_call" | custom-call | flops 8999999488 | bytes 14000000 | tf_op jit(solution)/shard_map/pallas_call | solution.py:448
  64.4 1.6 %shard_map.96 = (bf16[128,2560]{1,0:T(8,128)(2,1)}, bf16[1056,1024]{1,0:T(8,128)(2,1)}) custom-call(bf16[2,4,32,1280]{3,2,1,0:T(8,128)(2,1)S(1)} %get-tuple-element.8.refs_0_, bf16[4,16,640]{2,1,0:T(8,128)(2,1)S(1)} %get-tuple-element.9.refs_1_, s32[8,128]{1,0:T(8,128)S(1)} %get-tuple-element.10.refs_2_, bf16[1056,1024]{1,0:T(8,128)(2,1)S(1)} %get-tuple-element.11.refs_3_), custom_call_target="tpu_custom_call" | custom-call | flops 100000000 | bytes 6000000 | tf_op jit(solution)/shard_map/pallas_call | solution.py:502
